TPU v7x, 32 devices: a whole 2x2x4 slice. The times are simulated.
32 devices in a mesh: pw: 8 (over z, core), band: 4 (over y, x).
Axes of the slice: x: 2, y: 2, z: 4, core: 2. Of those that a mesh axis runs over, the one named last changes fastest.
Arguments:
- slab: bfloat16 [512, 2, 98304], P('band', None, 'pw'), may hold values from -0.01953125 to 0.01953125
- panel: float32 [16, 2, 98304], P('band', None, 'pw'), may hold values from -6 to 6
- potential: float32 [128, 128, 128], P('pw'), may hold values from -2 to 2
- pw_slot: int32 [98304], P('pw'), may hold values from 0 to 32767, as said below
- columns: int32 [2048], P('pw'), may hold values from 0 to 16383, as said below
Outputs:
- ritz_blocks: float32 [512, 64], P('band', 'pw')
Inputs may be any that keep to these rules, and one draw needn't show every extreme that they name: Entry d * 256 + s is the grid column i1 * 128 + i2 of column slot s of index d of pw; all entries are distinct, and together they are the columns nearest the grid's third axis. `pw_slot`: the rows held by index d of pw are distinct values c * 128 + i3: the plane wave at third index i3 of column slot c of index d; within each device they are the cells of its columns nearest the grid's anchor.
All inputs are finite; a program needn't handle non-finite values.
Results may differ from a plain program's by a relative error of at most 0.0029.
Values may be sent and summed in bfloat16 or wider, within the bound.
A program may use at most 128 MiB of HBM per device.

v0:
```python
import functools
import math

import jax
import jax.numpy as jnp
import numpy as np
from jax import lax
from jax.experimental import pallas as pl
from jax.experimental.pallas import tpu as pltpu
from jax.sharding import PartitionSpec as P

F32 = jnp.float32
BF16 = jnp.bfloat16
NT = (((1,), (1,)), ((), ()))
TN = (((0,), (0,)), ((), ()))


def round_up(value, step):
    return -(-value // step) * step


def disk_square(first_len, second_len, count):
    one = np.arange(first_len) - first_len // 2
    two = np.arange(second_len) - second_len // 2
    return int(np.sort((one[:, None] ** 2 + two[None, :] ** 2).ravel())[count - 1])


def window(half, step, length):
    return min(round_up(2 * (half + 1), step), length)


def cos_sin(rows, cols, length):
    angles = 2.0 * np.pi / length * ((rows[:, None] * cols[None, :]) % length)
    factor = 1.0 / math.sqrt(length)
    return np.cos(angles) * factor, np.sin(angles) * factor


def signed_of(width):
    return np.arange(width) - width // 2


def z_tables(count, length, planes, width):
    devices = length // planes
    cos, sin = cos_sin(signed_of(width), np.arange(length), length)
    cos = cos.reshape(width, devices, planes)
    sin = sin.reshape(width, devices, planes)
    table = np.zeros((count, 2, width, devices, 2, count, planes), np.float32)
    for k in range(count):
        table[k, 0, :, :, 0, k] = cos
        table[k, 1, :, :, 0, k] = -sin
        table[k, 0, :, :, 1, k] = sin
        table[k, 1, :, :, 1, k] = cos
    size = count * 2
    return table.reshape(size * width, devices * size * planes)


def scatter_kernel(length, width, slot_ref, panel_ref, table_ref, out_ref, acc):
    step = pl.program_id(0)

    @pl.when(step == 0)
    def _():
        acc[...] = jnp.zeros_like(acc)

    slot = slot_ref[...]
    block = slot.shape[1]
    cols = acc.shape[1]
    col = slot // length
    third = lax.rem(lax.rem(slot, length) + width // 2, length)
    pick_col = (lax.broadcasted_iota(jnp.int32, (cols, block), 0) == col).astype(F32).astype(BF16)
    pick_third = (
        (lax.broadcasted_iota(jnp.int32, (width, block), 0) == third).astype(F32).astype(BF16)
    )
    values = panel_ref[...].astype(BF16)
    spread = jnp.concatenate(
        [pick_third * values[q : q + 1] for q in range(values.shape[0])], axis=0
    )
    acc[...] += lax.dot_general(spread, pick_col, NT, preferred_element_type=F32)

    @pl.when(step == pl.num_programs(0) - 1)
    def _():
        lanes = out_ref.shape[2]
        got = acc[...].astype(BF16)
        done = lax.dot_general(got, table_ref[...], TN, preferred_element_type=F32).astype(BF16)
        for d in range(out_ref.shape[0]):
            out_ref[d] = done[:, d * lanes : (d + 1) * lanes]


def scatter_z(slot, rows, table, cols, length, width, devices):
    count, n = rows.shape
    block = 1024
    lanes = table.shape[1] // devices
    return pl.pallas_call(
        functools.partial(scatter_kernel, length, width),
        grid=(n // block,),
        in_specs=[
            pl.BlockSpec((1, block), lambda i: (0, i)),
            pl.BlockSpec((count, block), lambda i: (0, i)),
            pl.BlockSpec(table.shape, lambda i: (0, 0)),
        ],
        out_specs=pl.BlockSpec((devices, cols, lanes), lambda i: (0, 0, 0)),
        out_shape=jax.ShapeDtypeStruct((devices, cols, lanes), BF16),
        scratch_shapes=[pltpu.VMEM((count * width, cols), F32)],
        compiler_params=pltpu.CompilerParams(vmem_limit_bytes=48 * 1024 * 1024),
        name="scatter_z",
    )(slot, rows, table)


def turn(tile, sign):
    half = tile.shape[1] // 2
    return jnp.concatenate([tile[:, half:], tile[:, :half]], axis=1) * sign


def plane_kernel(
    wide, n_one, n_two, pos_ref, x_ref, ty_ref, tx_ref, txb_ref, tyb_ref, v_ref, out_ref,
    wave, box, mid, vbuf, sem,
):
    total, lanes = wave.shape
    copy = pltpu.make_async_copy(v_ref, vbuf, sem)
    copy.start()
    sign = jnp.where(
        lax.broadcasted_iota(jnp.int32, (1, lanes), 1) < lanes // 2, -1.0, 1.0
    ).astype(F32)
    wave[...] = x_ref[...].astype(F32)
    box[...] = jnp.zeros_like(box)

    def put(step, carry):
        for u in range(16):
            c = step * 16 + u
            box[pl.ds(pos_ref[c], 1), :] = wave[pl.ds(c, 1), :]
        return carry

    lax.fori_loop(0, total // 16, put, 0)

    def stacked(tiles):
        plain = jnp.concatenate(tiles, axis=1)
        turned = jnp.concatenate([turn(tile, sign) for tile in tiles], axis=1)
        return jnp.concatenate([plain, turned], axis=0).astype(BF16)

    def inverse_two(step, carry):
        tiles = [box[pl.ds(pl.multiple_of((2 * step + u) * wide, 8), wide), :] for u in range(2)]
        got = jnp.dot(ty_ref[...], stacked(tiles), preferred_element_type=F32)
        for u in range(2):
            mid[pl.ds(2 * step + u, n_two, stride=wide), :] = got[:, u * lanes : (u + 1) * lanes]
        return carry

    lax.fori_loop(0, wide // 2, inverse_two, 0, unroll=2)
    copy.wait()

    def both_one(step, carry):
        starts = [pl.multiple_of((2 * step + u) * wide, 8) for u in range(2)]
        tiles = [mid[pl.ds(start, wide), :] for start in starts]
        got = jnp.dot(tx_ref[...], stacked(tiles), preferred_element_type=F32)
        got = got * vbuf[:, pl.ds(pl.multiple_of(step * 2 * lanes, 2 * lanes), 2 * lanes)]
        tiles = [got[:, u * lanes : (u + 1) * lanes] for u in range(2)]
        back = jnp.dot(txb_ref[...], stacked(tiles), preferred_element_type=F32)
        for u in range(2):
            mid[pl.ds(starts[u], wide), :] = back[:, u * lanes : (u + 1) * lanes]
        return carry

    lax.fori_loop(0, n_two // 2, both_one, 0, unroll=2)

    def forward_two(step, carry):
        tiles = [mid[pl.ds(2 * step + u, n_two, stride=wide), :] for u in range(2)]
        got = jnp.dot(tyb_ref[...], stacked(tiles), preferred_element_type=F32)
        for u in range(2):
            start = pl.multiple_of((2 * step + u) * wide, 8)
            box[pl.ds(start, wide), :] = got[:, u * lanes : (u + 1) * lanes]
        return carry

    lax.fori_loop(0, wide // 2, forward_two, 0, unroll=2)

    def take(step, carry):
        for u in range(16):
            c = step * 16 + u
            wave[pl.ds(c, 1), :] = box[pl.ds(pos_ref[c], 1), :]
        return carry

    lax.fori_loop(0, total // 16, take, 0)
    out_ref[...] = wave[...].astype(BF16)


def plane_part(pos, x, tables, potential_rows, wide, n_one, n_two):
    total, lanes = x.shape
    whole = pl.BlockSpec(memory_space=pltpu.VMEM)
    return pl.pallas_call(
        functools.partial(plane_kernel, wide, n_one, n_two),
        in_specs=[pl.BlockSpec(memory_space=pltpu.SMEM)]
        + [whole] * 5
        + [pl.BlockSpec(memory_space=pl.ANY)],
        out_specs=whole,
        out_shape=jax.ShapeDtypeStruct((total, lanes), BF16),
        scratch_shapes=[
            pltpu.VMEM((total, lanes), F32),
            pltpu.VMEM((wide * wide, lanes), F32),
            pltpu.VMEM((n_two * wide, lanes), F32),
            pltpu.VMEM(potential_rows.shape, F32),
            pltpu.SemaphoreType.DMA,
        ],
        compiler_params=pltpu.CompilerParams(vmem_limit_bytes=56 * 1024 * 1024),
        name="plane_part",
    )(pos, x, *tables, potential_rows)


def gather_kernel(
    lengths, width, slot_ref, panel_ref, x_ref, table_ref, marks_ref, out_ref, held
):
    n_one, n_two, length = lengths
    count = panel_ref.shape[0]
    body = count * width

    @pl.when(pl.program_id(0) == 0)
    def _():
        x = jnp.concatenate([x_ref[d] for d in range(x_ref.shape[0])], axis=1)
        held[:body, :] = lax.dot_general(
            table_ref[...], x, NT, preferred_element_type=F32
        ).astype(BF16)
        held[body:, :] = marks_ref[...]

    slot = slot_ref[...]
    block = slot.shape[1]
    cols = held.shape[1]
    col = slot // length
    third = lax.rem(slot, length)
    place = lax.rem(third + width // 2, length)
    pick_col = (lax.broadcasted_iota(jnp.int32, (cols, block), 0) == col).astype(F32).astype(BF16)
    at_third = lax.broadcasted_iota(jnp.int32, (width, block), 0) == place
    got = jnp.dot(held[...], pick_col, preferred_element_type=F32)
    f_one = got[body : body + 1] * (2.0 / n_one)
    f_two = got[body + 1 : body + 2] * (2.0 / n_two)
    f_three = jnp.where(third < length // 2, third, third - length).astype(F32) * (2.0 / length)
    kinetic = 0.5 * (f_one * f_one + f_two * f_two + f_three * f_three)
    picked = jnp.concatenate(
        [
            jnp.sum(
                jnp.where(at_third, got[q * width : (q + 1) * width], 0.0), axis=0, keepdims=True
            )
            for q in range(count)
        ],
        axis=0,
    )
    out_ref[...] = (kinetic * panel_ref[...] + picked).astype(BF16)


def gather_z(slot, rows, x, table, marks, lengths, width):
    count, n = rows.shape
    devices, cols, lanes = x.shape
    block = 1024
    return pl.pallas_call(
        functools.partial(gather_kernel, lengths, width),
        grid=(n // block,),
        in_specs=[
            pl.BlockSpec((1, block), lambda i: (0, i)),
            pl.BlockSpec((count, block), lambda i: (0, i)),
            pl.BlockSpec(x.shape, lambda i: (0, 0, 0)),
            pl.BlockSpec(table.shape, lambda i: (0, 0)),
            pl.BlockSpec(marks.shape, lambda i: (0, 0)),
        ],
        out_specs=pl.BlockSpec((count, block), lambda i: (0, i)),
        out_shape=jax.ShapeDtypeStruct((count, n), BF16),
        scratch_shapes=[pltpu.VMEM((count * width + marks.shape[0], cols), BF16)],
        compiler_params=pltpu.CompilerParams(vmem_limit_bytes=48 * 1024 * 1024),
        name="gather_z",
    )(slot, rows, x, table, marks)


def signed_index(index, length):
    return jnp.where(index < length // 2, index, index - length)


def per_device(slab, panel, potential, pw_slot, columns):
    devices = lax.axis_size("pw")
    planes, n_one, n_two = potential.shape
    length = planes * devices
    cols = columns.shape[0]
    count = panel.shape[0]
    n = panel.shape[2]
    lanes = 2 * count * planes

    square = disk_square(n_one, n_two, cols * devices)
    wide = window(math.isqrt(square), 64, max(n_one, n_two))
    reach = math.isqrt(square + (-(-n // (2 * cols)) + 2) ** 2) + 1
    width = window(reach, 16, length)

    ztab = z_tables(count, length, planes, width)
    cy, sy = cos_sin(np.arange(n_two), signed_of(wide), n_two)
    cx, sx = cos_sin(np.arange(n_one), signed_of(wide), n_one)
    tables = [
        np.concatenate([cy, sy], axis=1),
        np.concatenate([cx, sx], axis=1),
        np.concatenate([cx.T, -sx.T], axis=1),
        np.concatenate([cy.T, -sy.T], axis=1),
    ]
    tables = [jnp.asarray(t, BF16) for t in tables]
    ztab = jnp.asarray(ztab, BF16)

    coeffs = panel.astype(BF16)
    rows = panel.reshape(2 * count, n)
    slot = pw_slot.reshape(1, n)

    every_column = lax.all_gather(columns, "pw", axis=0, tiled=True)
    place_one = signed_index(every_column // n_two, n_one) + wide // 2
    place_two = signed_index(every_column % n_two, n_two) + wide // 2
    pos = place_one * wide + place_two
    mine = jnp.stack(
        [signed_index(columns // n_two, n_one), signed_index(columns % n_two, n_two)], axis=0
    )
    marks = jnp.concatenate([mine, jnp.zeros((14, cols), jnp.int32)], axis=0).astype(BF16)
    potential_rows = jnp.tile(
        jnp.transpose(potential, (1, 2, 0)), (1, 1, 2 * count)
    ).reshape(n_one, n_two * lanes)

    every_coeff = lax.all_gather(coeffs, "band", axis=0, tiled=True)
    sent = scatter_z(slot, rows, ztab, cols, length, width, devices)
    there = lax.all_to_all(sent, "pw", split_axis=0, concat_axis=0, tiled=True)
    worked = plane_part(
        pos, there.reshape(devices * cols, lanes), tables, potential_rows, wide, n_one, n_two
    )
    home = lax.all_to_all(
        worked.reshape(devices, cols, lanes), "pw", split_axis=0, concat_axis=0, tiled=True
    )
    applied = gather_z(slot, rows, home, ztab, marks, (n_one, n_two, length), width)
    every_applied = lax.all_gather(
        applied.reshape(count, 2, n), "band", axis=0, tiled=True
    )

    def project(piece):
        terms = jnp.einsum("jcw,nqw->cjqn", slab, piece, preferred_element_type=F32)
        return jnp.concatenate(
            [terms[0, :, 0] + terms[1, :, 1], terms[0, :, 1] - terms[1, :, 0]], axis=1
        )

    blocks = jnp.concatenate([project(every_applied), project(every_coeff)], axis=1)
    return lax.psum_scatter(blocks, "pw", scatter_dimension=1, tiled=True)


def solution(mesh):
    in_specs = (P("band", None, "pw"), P("band", None, "pw"), P("pw", None, None), P("pw"), P("pw"))
    out_specs = P("band", "pw")
    return jax.shard_map(
        per_device, mesh=mesh, in_specs=in_specs, out_specs=out_specs, check_vma=False
    )
```

profile of v0, /device:TPU:0, one launch (start us, length us, event | category | flops | bytes accessed | tf_op | source)
XLA Modules:
  0.0 169.2 jit_solution(16192501763403720729)
XLA Ops:
  0.0 1.3 reshape.24.panel_ref
  1.3 0.0 copy-start
  1.3 1.3 copy-done
  2.6 0.0 copy-start.2
  2.6 0.8 copy-done.2
  3.4 8.2 %scatter_z.1 = bf16[8,256,128]{2,1,0:T(8,128)(2,1)} custom-call(s32[1,12288]{1,0:T(1,128)S(1)} %bitcast.40, f32[8,12288]{1,0:T(8,128)S(1)} %reshape.24.panel_ref, bf16[640,1024]{1,0:T(8,128)(2,1)S(1)} %copy-done), custom_call_target="tpu_custom_call" | custom-call | tf_op jit(solution)/shard_map/scatter_z/pallas_call | solution.py:92
  11.6 6.3 %all-to-all-start = ((bf16[8,256,128]{2,1,0:T(8,128)(2,1)}), bf16[8,256,128]{2,1,0:T(8,128)(2,1)S(1)}, u32[]{:S(2)}, u32[]{:S(2)}) async-start(bf16[8,256,128]{2,1,0:T(8,128)(2,1)} %scatter_z.1), calls=%async_computation | async-start | bytes 1048576 | tf_op jit(solution)/shard_map/all_to_all | solution.py:314
  17.9 1.1 convert_element_type.4
  19.1 1.7 %copy.28 = f32[128,128,16]{0,2,1:T(8,128)S(1)} copy(f32[128,128,16]{1,0,2:T(8,128)} %bitcast.45) | data formatting | bytes 2097152 | tf_op jit(solution)/shard_map/transpose | solution.py:309
  20.8 3.9 %tile.8 = f32[128,128,8,16]{0,3,2,1:T(8,128)} broadcast(f32[128,128,16]{0,2,1:T(8,128)S(1)} %copy.28), dimensions={0,1,3} | broadcast | bytes 9437184 | tf_op jit(solution)/shard_map/tile | solution.py:308
  24.7 0.0 copy-start.5
  24.7 0.0 copy-start.6
  24.7 9.0 %copy.29.v_ref = f32[128,16384]{1,0:T(8,128)} copy(f32[128,16384]{0,1:T(8,128)} %bitcast.42) | data formatting | bytes 16777216 | tf_op jit(solution)/shard_map/tile | solution.py:308
  33.7 0.0 copy-done.5
  33.8 0.1 pad.6.clone
  33.8 0.0 copy-done.6
  33.9 0.6 dynamic-slice
  35.1 12.2 %all-gather = s32[8,1,256]{2,1,0:T(1,128)S(1)} all-gather(s32[1,1,256]{2,1,0:T(1,128)S(1)} %bitcast.48), channel_id=1, replica_groups=mesh['pw'=8,'band'=4] {'pw'}, dimensions={0}, use_global_device_ids=true | all-gather | bytes 9216 | tf_op jit(solution)/shard_map/all_gather | solution.py:300
  47.3 12.4 %all_gather.11 = bf16[16,2,12288]{2,1,0:T(2,128)(2,1)S(1)} all-gather(bf16[4,2,12288]{2,1,0:T(2,128)(2,1)S(1)} %convert_element_type.4), channel_id=1, replica_groups=mesh['pw'=8,'band'=4] {'band'}, dimensions={0}, use_global_device_ids=true | all-gather | bytes 983040 | tf_op jit(solution)/shard_map/all_gather | solution.py:312
  59.7 0.6 fusion.16.pos_ref
  60.3 0.0 all-to-all-done
  60.3 0.0 copy-start.4
  60.3 0.8 copy-done.4
  61.2 33.4 %plane_part.1 = bf16[2048,128]{1,0:T(8,128)(2,1)} custom-call(s32[2048]{0:T(1024)} %fusion.16.pos_ref, bf16[2048,128]{1,0:T(8,128)(2,1)} %bitcast.43, bf16[128,128]{1,0:T(8,128)(2,1)} %constant.66.clone.ty_ref.tx_ref, bf16[128,128]{1,0:T(8,128)(2,1)} %constant.66.clone.ty_ref.tx_ref, bf16[64,256]{1,0:T(8,128)(2,1)} %constant.67.clone.txb_ref.tyb_ref, ...), custom_call_target="tpu_custom_call" | custom-call | tf_op jit(solution)/shard_map/plane_part/pallas_call | solution.py:185
  94.6 0.0 copy-start.1
  94.6 0.0 copy-start.3
  94.6 3.8 %all-to-all-start.1 = ((bf16[8,256,128]{2,1,0:T(8,128)(2,1)}), bf16[8,256,128]{2,1,0:T(8,128)(2,1)S(1)}, u32[]{:S(2)}, u32[]{:S(2)}) async-start(bf16[8,256,128]{2,1,0:T(8,128)(2,1)} %bitcast.44), calls=%async_computation.1 | async-start | bytes 1048576 | tf_op jit(solution)/shard_map/all_to_all | solution.py:318
  98.5 0.1 maximum_maximum_fusion.marks_ref
  98.5 10.2 %fusion.8 = f32[2,128,2,16]{1,3,2,0:T(8,128)S(1)} fusion(bf16[128,2,12288,1]{2,1,0,3:T(2,128)(2,1)} %bitcast.49, bf16[16,2,12288]{2,1,0:T(2,128)(2,1)S(1)} %all_gather.11), kind=kOutput, calls=%fused_computation.6 | convolution fusion | flops 201326592 | bytes 7110656 | tf_op jit(solution)/shard_map/jcw,nqw->cjqn/dot_general | solution.py:327
  108.7 4.8 %all-to-all-done.1.x_ref = bf16[8,256,128]{2,1,0:T(8,128)(2,1)S(1)} async-done(((bf16[8,256,128]{2,1,0:T(8,128)(2,1)}), bf16[8,256,128]{2,1,0:T(8,128)(2,1)S(1)}, u32[]{:S(2)}, u32[]{:S(2)}) %all-to-all-start.1) | async-done | bytes 524320 | tf_op jit(solution)/shard_map/all_to_all | solution.py:318
  113.6 0.0 copy-done.1
  113.6 0.0 copy-done.3
  113.6 7.3 %gather_z.1 = bf16[8,12288]{1,0:T(8,128)(2,1)S(1)} custom-call(s32[1,12288]{1,0:T(1,128)S(1)} %bitcast.41, f32[8,12288]{1,0:T(8,128)S(1)} %reshape.24.panel_ref, bf16[8,256,128]{2,1,0:T(8,128)(2,1)S(1)} %all-to-all-done.1.x_ref, bf16[640,1024]{1,0:T(8,128)(2,1)S(1)} %copy-done.1, bf16[16,256]{1,0:T(8,128)(2,1)S(1)} %maximum_maximum_fusion.marks_ref), custom_call_target="tpu_custom_call" | custom-call | tf_op jit(solution)/shard_map/gather_z/pallas_call | solution.py:248
  120.9 0.1 reshape.27
  121.0 11.4 %all_gather.10 = bf16[16,2,12288]{2,1,0:T(2,128)(2,1)S(1)} all-gather(bf16[4,2,12288]{2,1,0:T(2,128)(2,1)S(1)} %reshape.27), channel_id=1, replica_groups=mesh['pw'=8,'band'=4] {'band'}, dimensions={0}, use_global_device_ids=true | all-gather | bytes 983040 | tf_op jit(solution)/shard_map/all_gather | solution.py:322
  132.5 10.2 %fusion.5 = f32[2,128,2,16]{1,3,0,2:T(8,128)S(1)} fusion(bf16[128,2,12288]{2,1,0:T(2,128)(2,1)} %param.10, bf16[16,2,12288,1]{2,1,0,3:T(2,128)(2,1)S(1)} %bitcast.46), kind=kOutput, calls=%fused_computation.5 | convolution fusion | flops 201326592 | bytes 7110656 | tf_op jit(solution)/shard_map/jcw,nqw->cjqn/dot_general | solution.py:327
  142.7 25.9 %all-reduce = f32[128,64]{0,1:T(8,128)S(1)} all-reduce(f32[128,64]{0,1:T(8,128)S(1)} %pad_maximum_fusion), channel_id=2, replica_groups=mesh['pw'=8,'band'=4] {'pw'}, use_global_device_ids=true, to_apply=%region_0.1.clone | all-reduce | flops 8192 | bytes 65536
  168.6 0.6 constant_dynamic-slice_fusion
  (8 shorter events, 0.0 us)
Async XLA Ops:
  1.3 1.3 copy-start
  2.6 0.8 copy-start.2
  11.6 48.7 %all-to-all-start = ((bf16[8,256,128]{2,1,0:T(8,128)(2,1)}), bf16[8,256,128]{2,1,0:T(8,128)(2,1)S(1)}, u32[]{:S(2)}, u32[]{:S(2)}) async-start(bf16[8,256,128]{2,1,0:T(8,128)(2,1)} %scatter_z.1), calls=%async_computation | async-start | bytes 1048576 | tf_op jit(solution)/shard_map/all_to_all | solution.py:314
  24.7 9.0 %copy-start.5 = (s32[256]{0:T(256)S(1)}, s32[256]{0:T(256)}, u32[]{:S(2)}) copy-start(s32[256]{0:T(256)} %param.14) | copy-start | bytes 3076
  24.7 9.1 %copy-start.6 = (u32[32]{0:T(128)S(1)}, u32[32]{0:T(128)}, u32[]{:S(2)}) copy-start(u32[32]{0:T(128)} %constant.71) | copy-start | bytes 388
  60.3 0.8 copy-start.4
  94.6 18.9 %copy-start.1 = (bf16[640,1024]{1,0:T(8,128)(2,1)S(1)}, bf16[640,1024]{1,0:T(8,128)(2,1)}, u32[]{:S(2)}) copy-start(bf16[640,1024]{1,0:T(8,128)(2,1)} %constant.68.clone.table_ref) | copy-start | bytes 3932164
  94.6 18.9 %copy-start.3 = (s32[12288]{0:T(1024)S(1)}, s32[12288]{0:T(1024)}, u32[]{:S(2)}) copy-start(s32[12288]{0:T(1024)} %param.13) | copy-start | bytes 147460
  94.6 18.9 %all-to-all-start.1 = ((bf16[8,256,128]{2,1,0:T(8,128)(2,1)}), bf16[8,256,128]{2,1,0:T(8,128)(2,1)S(1)}, u32[]{:S(2)}, u32[]{:S(2)}) async-start(bf16[8,256,128]{2,1,0:T(8,128)(2,1)} %bitcast.44), calls=%async_computation.1 | async-start | bytes 1048576 | tf_op jit(solution)/shard_map/all_to_all | solution.py:318
where the time goes:
time: 170 us; the launch traced here: 169 us
  blocking collectives  62 us (36%)
  Pallas kernels  48.9 us (29%)
  local copies, waits for them, and re-layouts  20.3 us (12%)
  matrix products  20.3 us (12%)
  starting transfers between devices  10.1 us (6%)
  waiting for transfers between devices  4.84 us (3%)
  other arithmetic  1.85 us (1%)
    pallas_call x1, Pallas kernels, plane_part(): pl.pallas_call(functools.partial(plane_kernel, wide, n_one, n_two), in_sp...  33.4 us
    unnamed x1, blocking collectives  25.9 us
    dot_general x2, matrix products, project(): terms = jnp.einsum('jcw,nqw->cjqn', slab, piece, preferred_element_type=F32)  20.3 us
    another operation x2, local copies, waits for them, and re-layouts, per_device(): jnp.tile(jnp.transpose(potential, (1, 2, 0)), (1, 1, 2 * count))  12.9 us
    all_gather x1, blocking collectives, per_device(): every_coeff = lax.all_gather(coeffs, 'band', axis=0, tiled=True)  12.4 us
    all_gather x1, blocking collectives, per_device(): every_column = lax.all_gather(columns, 'pw', axis=0, tiled=True)  12.2 us
    all_gather x1, blocking collectives, per_device(): lax.all_gather(applied.reshape(count, 2, n), 'band', axis=0, tiled=True)  11.4 us
    pallas_call x1, Pallas kernels, scatter_z(): pl.pallas_call(functools.partial(scatter_kernel, length, width), grid=(n...  8.21 us
  transfers between devices with their start and end apart: 2, of which 1 were waited for; matrix products, arithmetic and copies ran while one was open for 16% of the time, Pallas kernels for 0%

commit v1 on v0

v1 whole, which is shorter than its diff:
```python
import functools
import math

import jax
import jax.numpy as jnp
import numpy as np
from jax import lax
from jax.experimental import pallas as pl
from jax.experimental.pallas import tpu as pltpu
from jax.sharding import PartitionSpec as P

F32 = jnp.float32
BF16 = jnp.bfloat16
NT = (((1,), (1,)), ((), ()))
TN = (((0,), (0,)), ((), ()))
MESH = pl.DeviceIdType.MESH
BLOCK = 1024
LIMIT = 56 * 1024 * 1024


def round_up(value, step):
    return -(-value // step) * step


def disk_square(first_len, second_len, count):
    one = np.arange(first_len) - first_len // 2
    two = np.arange(second_len) - second_len // 2
    return int(np.sort((one[:, None] ** 2 + two[None, :] ** 2).ravel())[count - 1])


def window(half, step, length):
    return min(round_up(2 * (half + 1), step), length)


def odd_tiles(width):
    return width if (width // 8) % 2 else width + 8


def cos_sin(rows, cols, length):
    angles = 2.0 * np.pi / length * ((rows[:, None] * cols[None, :]) % length)
    factor = 1.0 / math.sqrt(length)
    return np.cos(angles) * factor, np.sin(angles) * factor


def signed_of(width):
    return np.arange(width) - width // 2


def z_tables(count, length, planes, width):
    devices = length // planes
    cos, sin = cos_sin(signed_of(width), np.arange(length), length)
    cos = cos.reshape(width, devices, planes)
    sin = sin.reshape(width, devices, planes)
    table = np.zeros((2, count, width, devices, 2, count, planes), np.float32)
    for k in range(count):
        table[0, k, :, :, 0, k] = cos
        table[1, k, :, :, 0, k] = -sin
        table[0, k, :, :, 1, k] = sin
        table[1, k, :, :, 1, k] = cos
    size = count * 2
    return table.reshape(size * width, devices * size * planes)


def peers_of(axis):
    size = lax.axis_size(axis)
    me = lax.axis_index(axis)
    return me, [lax.rem(me + off, size) for off in range(1, size)]


def greet(axes):
    barrier = pltpu.get_barrier_semaphore()
    waits = 0
    for axis in axes:
        for peer in peers_of(axis)[1]:
            pl.semaphore_signal(barrier, inc=1, device_id={axis: peer}, device_id_type=MESH)
            waits += 1
    pl.semaphore_wait(barrier, waits)


def send_to(axis, peer, src, dst, send_sem, recv_sem):
    copy = pltpu.make_async_remote_copy(
        src_ref=src,
        dst_ref=dst,
        send_sem=send_sem,
        recv_sem=recv_sem,
        device_id={axis: peer},
        device_id_type=MESH,
    )
    copy.start()
    return copy


def arrived(axis, peer, dst, send_sem, recv_sem):
    pltpu.make_async_remote_copy(
        src_ref=dst,
        dst_ref=dst,
        send_sem=send_sem,
        recv_sem=recv_sem,
        device_id={axis: peer},
        device_id_type=MESH,
    ).wait_recv()


def packed(rows):
    half = rows.shape[1] // 2
    return jnp.concatenate([rows[:, :half], rows[:, half:]], axis=0).astype(BF16)


def unpacked(tile):
    half = tile.shape[0] // 2
    return jnp.concatenate([tile[:half], tile[half:]], axis=1)


def panel_rows(panel_ref, start):
    count = panel_ref.shape[0]
    pairs = [panel_ref[k, :, pl.ds(start, BLOCK)] for k in range(count)]
    return jnp.concatenate(
        [pair[0:1] for pair in pairs] + [pair[1:2] for pair in pairs], axis=0
    )


def one_hot(size, places):
    grid = lax.broadcasted_iota(jnp.int32, (size, places.shape[1]), 0)
    return (grid == places).astype(F32).astype(BF16)


def first_kernel(
    length, width, slot_ref, panel_ref, columns_ref, table_ref, out_ref, cols_ref, coef_ref,
    acc, stage, land, cols_land, coef_land, send_x, recv_x, send_c, recv_c, send_b, recv_b,
):
    me, others = peers_of("pw")
    here, mates = peers_of("band")
    steps = slot_ref.shape[1] // BLOCK
    lanes = land.shape[2]
    cols = acc.shape[1]
    greet(("pw", "band"))

    def pack(step, carry):
        start = pl.multiple_of(step * BLOCK, BLOCK)
        coef_land[here, step] = packed(panel_rows(panel_ref, start))
        return carry

    lax.fori_loop(0, steps, pack, 0)
    cols_land[me] = columns_ref[...]
    copies = []
    for peer in others:
        copies.append(
            send_to("pw", peer, columns_ref, cols_land.at[me], send_c.at[peer], recv_c.at[me])
        )
    for mate in mates:
        copies.append(
            send_to(
                "band", mate, coef_land.at[here], coef_land.at[here], send_b.at[mate],
                recv_b.at[here],
            )
        )
    acc[...] = jnp.zeros_like(acc)

    def scatter(step, carry):
        start = pl.multiple_of(step * BLOCK, BLOCK)
        slot = slot_ref[:, pl.ds(start, BLOCK)]
        third = lax.rem(lax.rem(slot, length) + width // 2, length)
        pick_col = one_hot(cols, slot // length)
        pick_third = one_hot(width, third)
        values = panel_rows(panel_ref, start).astype(BF16)
        spread = jnp.concatenate(
            [pick_third * values[q : q + 1] for q in range(values.shape[0])], axis=0
        )
        acc[...] += lax.dot_general(spread, pick_col, NT, preferred_element_type=F32)
        return carry

    lax.fori_loop(0, steps, scatter, 0)
    got = acc[...].astype(BF16)
    done = lax.dot_general(got, table_ref[...], TN, preferred_element_type=F32).astype(BF16)
    for d in range(land.shape[0]):
        stage[d] = done[:, d * lanes : (d + 1) * lanes]
    for peer in others:
        copies.append(
            send_to("pw", peer, stage.at[peer], land.at[me], send_x.at[peer], recv_x.at[me])
        )
    land[me] = stage[me]
    for peer in others:
        arrived("pw", peer, cols_land.at[peer], send_c.at[peer], recv_c.at[peer])
    for mate in mates:
        arrived("band", mate, coef_land.at[mate], send_b.at[mate], recv_b.at[mate])
    cols_ref[...] = cols_land[...]
    coef_ref[...] = coef_land[...]
    for peer in others:
        arrived("pw", peer, land.at[peer], send_x.at[peer], recv_x.at[peer])
    out_ref[...] = land[...]
    for copy in copies:
        copy.wait_send()


def first_part(slot, panel, columns, table, length, width, devices, mates):
    count, _, n = panel.shape
    cols = columns.shape[1]
    lanes = table.shape[1] // devices
    whole = pl.BlockSpec(memory_space=pltpu.VMEM)
    coef_shape = (mates, n // BLOCK, 4 * count, BLOCK // 2)
    dma = pltpu.SemaphoreType.DMA
    return pl.pallas_call(
        functools.partial(first_kernel, length, width),
        in_specs=[whole] * 4,
        out_specs=[whole] * 3,
        out_shape=[
            jax.ShapeDtypeStruct((devices, cols, lanes), BF16),
            jax.ShapeDtypeStruct((devices, 1, cols), jnp.int32),
            jax.ShapeDtypeStruct(coef_shape, BF16),
        ],
        scratch_shapes=[
            pltpu.VMEM((2 * count * width, cols), F32),
            pltpu.VMEM((devices, cols, lanes), BF16),
            pltpu.VMEM((devices, cols, lanes), BF16),
            pltpu.VMEM((devices, 1, cols), jnp.int32),
            pltpu.VMEM(coef_shape, BF16),
            dma((devices,)),
            dma((devices,)),
            dma((devices,)),
            dma((devices,)),
            dma((mates,)),
            dma((mates,)),
        ],
        compiler_params=pltpu.CompilerParams(
            vmem_limit_bytes=LIMIT, collective_id=1, has_side_effects=True
        ),
        name="first_part",
    )(slot, panel, columns, table)


def plane_kernel(
    wide, n_one, n_two, pos_ref, x_ref, tx_ref, ty_ref, tyb_ref, txb_ref, v_ref, out_ref,
    wave, box, mid, mid_back,
):
    total, lanes = wave.shape
    planes = v_ref.shape[0] // n_one
    sign = jnp.where(
        lax.broadcasted_iota(jnp.int32, (1, lanes), 1) < lanes // 2, -1.0, 1.0
    ).astype(F32)
    wave[...] = x_ref[...].astype(F32)
    box[...] = jnp.zeros_like(box)
    group = 16

    def put(step, carry):
        base = pl.multiple_of(step * group, group)
        tile = wave[pl.ds(base, group), :]
        for u in range(group):
            box[pl.ds(pos_ref[base + u], 1), :] = tile[u : u + 1]
        return carry

    lax.fori_loop(0, total // group, put, 0)

    def stacked(tiles):
        plain = jnp.concatenate(tiles, axis=1)
        turned = jnp.concatenate(
            [pltpu.roll(tile, lanes // 2, 1) * sign for tile in tiles], axis=1
        )
        return jnp.concatenate([plain, turned], axis=0).astype(BF16)

    def split(got):
        return [got[:, u * lanes : (u + 1) * lanes] for u in range(got.shape[1] // lanes)]

    def inverse_one(step, carry):
        tiles = [box[pl.ds(pl.multiple_of((2 * step + u) * wide, 8), wide), :] for u in range(2)]
        got = jnp.dot(tx_ref[...], stacked(tiles), preferred_element_type=F32)
        for u, tile in enumerate(split(got)):
            mid[pl.ds(2 * step + u, n_one, stride=wide), :] = tile
        return carry

    lax.fori_loop(0, wide // 2, inverse_one, 0, unroll=4)

    def both_two(step, carry):
        starts = [pl.multiple_of((2 * step + u) * wide, 8) for u in range(2)]
        tiles = [mid[pl.ds(start, wide), :] for start in starts]
        got = jnp.dot(ty_ref[...], stacked(tiles), preferred_element_type=F32)
        tiles = []
        for u, tile in enumerate(split(got)):
            local = v_ref[pl.ds(2 * step + u, planes, stride=n_one), :]
            tiles.append(tile * jnp.concatenate([local] * (lanes // planes), axis=0).T)
        back = jnp.dot(tyb_ref[...], stacked(tiles), preferred_element_type=F32)
        for u, tile in enumerate(split(back)):
            mid_back[pl.ds(starts[u], wide), :] = tile
        return carry

    lax.fori_loop(0, n_one // 2, both_two, 0, unroll=4)

    def forward_one(step, carry):
        tiles = [mid_back[pl.ds(2 * step + u, n_one, stride=wide), :] for u in range(2)]
        got = jnp.dot(txb_ref[...], stacked(tiles), preferred_element_type=F32)
        for u, tile in enumerate(split(got)):
            start = pl.multiple_of((2 * step + u) * wide, 8)
            box[pl.ds(start, wide), :] = tile
        return carry

    lax.fori_loop(0, wide // 2, forward_one, 0, unroll=4)

    def take(step, carry):
        base = pl.multiple_of(step * group, group)
        rows = [box[pl.ds(pos_ref[base + u], 1), :] for u in range(group)]
        for u in range(group):
            wave[pl.ds(base + u, 1), :] = rows[u]
        return carry

    lax.fori_loop(0, total // group, take, 0)
    out_ref[...] = wave[...].astype(BF16)


def plane_part(pos, x, tables, potential_rows, wide, n_one, n_two):
    total, lanes = x.shape
    whole = pl.BlockSpec(memory_space=pltpu.VMEM)
    return pl.pallas_call(
        functools.partial(plane_kernel, wide, n_one, n_two),
        in_specs=[pl.BlockSpec(memory_space=pltpu.SMEM)] + [whole] * 6,
        out_specs=whole,
        out_shape=jax.ShapeDtypeStruct((total, lanes), BF16),
        scratch_shapes=[
            pltpu.VMEM((total, lanes), F32),
            pltpu.VMEM((wide * wide, lanes), F32),
            pltpu.VMEM((n_one * wide, lanes), F32),
            pltpu.VMEM((n_one * wide, lanes), F32),
        ],
        compiler_params=pltpu.CompilerParams(vmem_limit_bytes=LIMIT),
        name="plane_part",
    )(pos, x, *tables, potential_rows)


def last_kernel(
    lengths, width, groups, slot_ref, panel_ref, x_ref, table_ref, marks_ref, coef_ref, slab_ref,
    out_ref, home, held, app, slab_in, slab_rows, acc_h, acc_m, terms, part, parts,
    slab_sem, send_x, recv_x, send_b, recv_b, send_p, recv_p,
):
    n_one, n_two, length = lengths
    me, others = peers_of("pw")
    here, mates = peers_of("band")
    bands = len(mates) + 1
    size = 2 * panel_ref.shape[0]
    body = size * width
    cols = held.shape[1]
    steps = slot_ref.shape[1] // BLOCK
    each = steps // groups
    fetch = pltpu.make_async_copy(slab_ref, slab_in, slab_sem)
    fetch.start()
    greet(("pw", "band"))
    copies = [
        send_to("pw", peer, x_ref.at[peer], home.at[me], send_x.at[peer], recv_x.at[me])
        for peer in others
    ]
    home[me] = x_ref[me]
    held[body:, :] = marks_ref[...]
    acc_h[...] = jnp.zeros_like(acc_h)
    acc_m[...] = jnp.zeros_like(acc_m)
    fetch.wait()

    def project(acc, slab_tile, ref, step):
        right = jnp.concatenate([unpacked(ref[b, step]) for b in range(bands)], axis=0)
        acc[...] += lax.dot_general(slab_tile, right, NT, preferred_element_type=F32)

    def margin(step, carry):
        start = pl.multiple_of(step * BLOCK, BLOCK)
        tile = slab_in[:, :, pl.ds(start, BLOCK)].reshape(slab_rows.shape[0], BLOCK)
        slab_rows[:, pl.ds(start, BLOCK)] = tile
        project(acc_m, tile, coef_ref, step)
        return carry

    lax.fori_loop(0, steps, margin, 0)
    for peer in others:
        arrived("pw", peer, home.at[peer], send_x.at[peer], recv_x.at[peer])
    x = jnp.concatenate([home[d] for d in range(home.shape[0])], axis=1)
    held[:body, :] = lax.dot_general(
        table_ref[...], x, NT, preferred_element_type=F32
    ).astype(BF16)

    def gather(step, carry):
        start = pl.multiple_of(step * BLOCK, BLOCK)
        slot = slot_ref[:, pl.ds(start, BLOCK)]
        third = lax.rem(slot, length)
        place = lax.rem(third + width // 2, length)
        pick_col = one_hot(cols, slot // length)
        at_third = lax.broadcasted_iota(jnp.int32, (width, BLOCK), 0) == place
        got = jnp.dot(held[...], pick_col, preferred_element_type=F32)
        f_one = got[body : body + 1] * (2.0 / n_one)
        f_two = got[body + 1 : body + 2] * (2.0 / n_two)
        signed = jnp.where(third < length // 2, third, third - length)
        f_three = signed.astype(F32) * (2.0 / length)
        kinetic = 0.5 * (f_one * f_one + f_two * f_two + f_three * f_three)
        picked = jnp.concatenate(
            [
                jnp.sum(
                    jnp.where(at_third, got[q * width : (q + 1) * width], 0.0),
                    axis=0,
                    keepdims=True,
                )
                for q in range(size)
            ],
            axis=0,
        )
        app[here, step] = packed(kinetic * panel_rows(panel_ref, start) + picked)
        return carry

    for g in range(groups):
        lax.fori_loop(g * each, (g + 1) * each, gather, 0)
        span = pl.ds(g * each, each)
        for mate in mates:
            copies.append(
                send_to(
                    "band", mate, app.at[here, span], app.at[here, span],
                    send_b.at[mate, g], recv_b.at[here, g],
                )
            )

    def hamiltonian(step, carry):
        start = pl.multiple_of(step * BLOCK, BLOCK)
        project(acc_h, slab_rows[:, pl.ds(start, BLOCK)], app, step)
        return carry

    for g in range(groups):
        span = pl.ds(g * each, each)
        for mate in mates:
            arrived("band", mate, app.at[mate, span], send_b.at[mate, g], recv_b.at[mate, g])
        lax.fori_loop(g * each, (g + 1) * each, hamiltonian, 0)

    terms[...] = jnp.concatenate([acc_h[...], acc_m[...]], axis=1)
    rows = terms.shape[0] // 2
    real_rows = terms[pl.ds(0, rows, stride=2), :].T
    imag_rows = terms[pl.ds(1, rows, stride=2), :].T

    def pick(value, kind, which):
        first = kind * bands * size + which * (size // 2)
        return jnp.concatenate(
            [value[first + b * size : first + b * size + size // 2] for b in range(bands)], axis=0
        )

    pieces = []
    for kind in range(2):
        pieces.append(pick(real_rows, kind, 0) + pick(imag_rows, kind, 1))
        pieces.append(pick(real_rows, kind, 1) - pick(imag_rows, kind, 0))
    part[...] = jnp.concatenate(pieces, axis=0)
    share = out_ref.shape[0]

    def block_of(index):
        return pl.ds(pl.multiple_of(index * share, share), share)

    for peer in others:
        copies.append(
            send_to(
                "pw", peer, part.at[block_of(peer)], parts.at[me], send_p.at[peer], recv_p.at[me]
            )
        )
    parts[me] = part[block_of(me), :]
    for peer in others:
        arrived("pw", peer, parts.at[peer], send_p.at[peer], recv_p.at[peer])
    total = parts[0]
    for d in range(1, parts.shape[0]):
        total = total + parts[d]
    out_ref[...] = total
    for copy in copies:
        copy.wait_send()


def last_part(slot, panel, x, table, marks, coef, slab, lengths, width):
    devices, cols, lanes = x.shape
    count, _, n = panel.shape
    mates = coef.shape[0]
    size = 2 * count
    rows = slab.shape[0]
    groups = 3 if (n // BLOCK) % 3 == 0 else 1
    share = 2 * mates * size // devices
    whole = pl.BlockSpec(memory_space=pltpu.VMEM)
    dma = pltpu.SemaphoreType.DMA
    return pl.pallas_call(
        functools.partial(last_kernel, lengths, width, groups),
        in_specs=[whole] * 6 + [pl.BlockSpec(memory_space=pl.ANY)],
        out_specs=whole,
        out_shape=jax.ShapeDtypeStruct((share, rows), F32),
        scratch_shapes=[
            pltpu.VMEM((devices, cols, lanes), BF16),
            pltpu.VMEM((size * width + marks.shape[0], cols), BF16),
            pltpu.VMEM(coef.shape, BF16),
            pltpu.VMEM(slab.shape, BF16),
            pltpu.VMEM((2 * rows, n), BF16),
            pltpu.VMEM((2 * rows, mates * size), F32),
            pltpu.VMEM((2 * rows, mates * size), F32),
            pltpu.VMEM((2 * rows, 2 * mates * size), F32),
            pltpu.VMEM((2 * mates * size, rows), F32),
            pltpu.VMEM((devices, share, rows), F32),
            dma,
            dma((devices,)),
            dma((devices,)),
            dma((mates, groups)),
            dma((mates, groups)),
            dma((devices,)),
            dma((devices,)),
        ],
        compiler_params=pltpu.CompilerParams(
            vmem_limit_bytes=LIMIT, collective_id=2, has_side_effects=True
        ),
        name="last_part",
    )(slot, panel, x, table, marks, coef, slab)


def signed_index(index, length):
    return jnp.where(index < length // 2, index, index - length)


def per_device(slab, panel, potential, pw_slot, columns):
    devices = lax.axis_size("pw")
    mates = lax.axis_size("band")
    planes, n_one, n_two = potential.shape
    length = planes * devices
    cols = columns.shape[0]
    count = panel.shape[0]
    n = panel.shape[2]
    lanes = 2 * count * planes

    square = disk_square(n_one, n_two, cols * devices)
    wide = odd_tiles(window(math.isqrt(square), 8, max(n_one, n_two)))
    reach = math.isqrt(square + (-(-n // (2 * cols)) + 2) ** 2) + 1
    width = window(reach, 16, length)

    ztab = jnp.asarray(z_tables(count, length, planes, width), BF16)
    cy, sy = cos_sin(np.arange(n_two), signed_of(wide), n_two)
    cx, sx = cos_sin(np.arange(n_one), signed_of(wide), n_one)
    tables = [
        np.concatenate([cx, sx], axis=1),
        np.concatenate([cy, sy], axis=1),
        np.concatenate([cy.T, -sy.T], axis=1),
        np.concatenate([cx.T, -sx.T], axis=1),
    ]
    tables = [jnp.asarray(t, BF16) for t in tables]

    slot = pw_slot.reshape(1, n)
    mine = jnp.stack(
        [signed_index(columns // n_two, n_one), signed_index(columns % n_two, n_two)], axis=0
    )
    marks = jnp.concatenate([mine, jnp.zeros((14, cols), jnp.int32)], axis=0).astype(BF16)

    there, every_column, coef = first_part(
        slot, panel, columns.reshape(1, cols), ztab, length, width, devices, mates
    )
    every_column = every_column.reshape(devices * cols)
    place_one = signed_index(every_column // n_two, n_one) + wide // 2
    place_two = signed_index(every_column % n_two, n_two) + wide // 2
    worked = plane_part(
        place_two * wide + place_one,
        there.reshape(devices * cols, lanes),
        tables,
        potential.reshape(planes * n_one, n_two),
        wide,
        n_one,
        n_two,
    )
    out = last_part(
        slot,
        panel,
        worked.reshape(devices, cols, lanes),
        ztab,
        marks,
        coef,
        slab,
        (n_one, n_two, length),
        width,
    )
    return out.T


def solution(mesh):
    in_specs = (P("band", None, "pw"), P("band", None, "pw"), P("pw", None, None), P("pw"), P("pw"))
    out_specs = P("band", "pw")
    return jax.shard_map(
        per_device, mesh=mesh, in_specs=in_specs, out_specs=out_specs, check_vma=False
    )
```

time: 170 us -> 89.7 us (0.53)
  blocking collectives: 62 us -> 0 us
  Pallas kernels: 48.9 us -> 85.4 us
  matrix products: 20.3 us -> 0 us
  local copies, waits for them, and re-layouts: 20.3 us -> 1.37 us
  starting transfers between devices: 10.1 us -> 0 us
  waiting for transfers between devices: 4.84 us -> 0 us
    pallas_call x2, Pallas kernels: 15.5 us -> 64.6 us  [the longest x1 39 us: last_part(): pl.pallas_call(functools.partial(last_kernel, lengths, width, groups), in...]
    all_gather x3 -> x0, blocking collectives: 36.1 us -> none  [the longest x1 12.4 us: per_device(): every_coeff = lax.all_gather(coeffs, 'band', axis=0, tiled=True)]
    unnamed x1 -> x0, blocking collectives: 25.9 us -> none
    dot_general x2 -> x0, matrix products: 20.3 us -> none  [project(): terms = jnp.einsum('jcw,nqw->cjqn', slab, piece, preferred_element_type=F32)]
    another operation x2 -> x0, local copies, waits for them, and re-layouts: 12.9 us -> none  [per_device(): jnp.tile(jnp.transpose(potential, (1, 2, 0)), (1, 1, 2 * count))]
    pallas_call x1, Pallas kernels: 33.4 us -> 20.8 us  [plane_part(): pl.pallas_call(functools.partial(plane_kernel, wide, n_one, n_two), in_sp...]
    all_to_all x2 -> x0, starting transfers between devices: 10.1 us -> none  [the longest x1 6.32 us: per_device(): there = lax.all_to_all(sent, 'pw', split_axis=0, concat_axis=0, tiled=True)]
    all_to_all x2 -> x0, waiting for transfers between devices: 4.84 us -> none  [the longest x1 4.84 us: per_device(): lax.all_to_all(worked.reshape(devices, cols, lanes), 'pw', split_axis=0,...]
  transfers between devices with their start and end apart: 2 -> 0, of which waited for: 1 -> 0; matrix products, arithmetic and copies ran while one was open for 16% -> 0% of each run, Pallas kernels for 0% -> 0%
where the time goes in v1:
time: 89.7 us; the launch traced here: 89.5 us
  Pallas kernels  85.4 us (95%)
  other arithmetic  2.66 us (3%)
  local copies, waits for them, and re-layouts  1.37 us (2%)
    pallas_call x1, Pallas kernels, last_part(): pl.pallas_call(functools.partial(last_kernel, lengths, width, groups), in...  39 us
    pallas_call x1, Pallas kernels, first_part(): pl.pallas_call(functools.partial(first_kernel, length, width), in_specs=[...  25.6 us
    pallas_call x1, Pallas kernels, plane_part(): pl.pallas_call(functools.partial(plane_kernel, wide, n_one, n_two), in_sp...  20.8 us

profile of v1, /device:TPU:0, one launch (start us, length us, event | category | flops | bytes accessed | tf_op | source)
XLA Modules:
  0.0 89.5 jit_solution(13861093080753037765)
XLA Ops:
  0.0 25.6 %first_part.1 = (bf16[8,256,128]{2,1,0:T(8,128)(2,1)}, s32[8,1,256]{2,1,0:T(1,128)}, bf16[4,12,16,512]{3,2,1,0:T(8,128)(2,1)}) custom-call(s32[1,12288]{1,0:T(1,128)} %bitcast.10, f32[4,2,12288]{2,1,0:T(2,128)} %panel_ref.3, s32[1,256]{1,0:T(1,128)} %bitcast.14, bf16[640,1024]{1,0:T(8,128)(2,1)} %constant.68.clone.table_ref), custom_call_target="tpu_custom_call" | custom-call | tf_op jit(solution)/shard_map/first_part/pallas_call | solution.py:202
  25.6 1.3 %fusion.2.pos_ref = s32[2048]{0:T(1024)} fusion(s32[2048]{0:T(1024)} %bitcast.13), kind=kLoop, calls=%fused_computation.9 | loop fusion | flops 59392 | bytes 16384 | tf_op jit(solution)/shard_map/add | solution.py:544
  26.9 20.8 %plane_part.1 = bf16[2048,128]{1,0:T(8,128)(2,1)} custom-call(s32[2048]{0:T(1024)} %fusion.2.pos_ref, bf16[2048,128]{1,0:T(8,128)(2,1)} %bitcast.9, bf16[128,112]{1,0:T(8,128)(2,1)} %constant.69.clone.tx_ref.ty_ref, bf16[128,112]{1,0:T(8,128)(2,1)} %constant.69.clone.tx_ref.ty_ref, bf16[56,256]{1,0:T(8,128)(2,1)} %constant.70.clone.tyb_ref.txb_ref, ...), custom_call_target="tpu_custom_call" | custom-call | tf_op jit(solution)/shard_map/plane_part/pallas_call | solution.py:311
  47.7 0.7 fusion.8
  48.4 0.1 pad.2.clone
  48.5 0.7 maximum_maximum_fusion.marks_ref
  49.2 39.0 %last_part.1 = f32[8,128]{1,0:T(8,128)} custom-call(s32[1,12288]{1,0:T(1,128)} %bitcast.11, f32[4,2,12288]{2,1,0:T(2,128)} %panel_ref.3, bf16[8,256,128]{2,1,0:T(8,128)(2,1)} %bitcast.7, bf16[640,1024]{1,0:T(8,128)(2,1)} %constant.68.clone.table_ref, bf16[16,256]{1,0:T(8,128)(2,1)} %maximum_maximum_fusion.marks_ref, ...), custom_call_target="tpu_custom_call" | custom-call | tf_op jit(solution)/shard_map/last_part/pallas_call | solution.py:470
  88.2 1.3 %copy.12 = f32[128,8]{0,1:T(8,128)} copy(f32[128,8]{0,1:T(8,128)} %bitcast.12) | data formatting | bytes 8192
  (3 shorter events, 0.0 us)

commit v2 on v1

v2 whole, which is shorter than its diff:
```python
import functools
import math

import jax
import jax.numpy as jnp
import numpy as np
from jax import lax
from jax.experimental import pallas as pl
from jax.experimental.pallas import tpu as pltpu
from jax.sharding import PartitionSpec as P

F32 = jnp.float32
BF16 = jnp.bfloat16
NT = (((1,), (1,)), ((), ()))
TN = (((0,), (0,)), ((), ()))
MESH = pl.DeviceIdType.MESH
BLOCK = 1024
LIMIT = 56 * 1024 * 1024


def round_up(value, step):
    return -(-value // step) * step


def disk_square(first_len, second_len, count):
    one = np.arange(first_len) - first_len // 2
    two = np.arange(second_len) - second_len // 2
    return int(np.sort((one[:, None] ** 2 + two[None, :] ** 2).ravel())[count - 1])


def window(half, step, length):
    return min(round_up(2 * (half + 1), step), length)


def odd_tiles(width):
    return width if (width // 8) % 2 else width + 8


def cos_sin(rows, cols, length):
    angles = 2.0 * np.pi / length * ((rows[:, None] * cols[None, :]) % length)
    factor = 1.0 / math.sqrt(length)
    return np.cos(angles) * factor, np.sin(angles) * factor


def signed_of(width):
    return np.arange(width) - width // 2


def z_tables(count, length, planes, width):
    devices = length // planes
    cos, sin = cos_sin(signed_of(width), np.arange(length), length)
    cos = cos.reshape(width, devices, planes)
    sin = sin.reshape(width, devices, planes)
    table = np.zeros((2, count, width, devices, 2, count, planes), np.float32)
    for k in range(count):
        table[0, k, :, :, 0, k] = cos
        table[1, k, :, :, 0, k] = -sin
        table[0, k, :, :, 1, k] = sin
        table[1, k, :, :, 1, k] = cos
    size = count * 2
    return table.reshape(size * width, devices * size * planes)


def peers_of(axis):
    size = lax.axis_size(axis)
    me = lax.axis_index(axis)
    offs = sorted(range(1, size), key=lambda off: abs(2 * off - size))
    return me, [lax.rem(me + off, size) for off in offs]


def greet(axes):
    barrier = pltpu.get_barrier_semaphore()
    waits = 0
    for axis in axes:
        for peer in peers_of(axis)[1]:
            pl.semaphore_signal(barrier, inc=1, device_id={axis: peer}, device_id_type=MESH)
            waits += 1
    pl.semaphore_wait(barrier, waits)


def send_to(axis, peer, src, dst, send_sem, recv_sem):
    copy = pltpu.make_async_remote_copy(
        src_ref=src,
        dst_ref=dst,
        send_sem=send_sem,
        recv_sem=recv_sem,
        device_id={axis: peer},
        device_id_type=MESH,
    )
    copy.start()
    return copy


def arrived(axis, peer, dst, send_sem, recv_sem):
    pltpu.make_async_remote_copy(
        src_ref=dst,
        dst_ref=dst,
        send_sem=send_sem,
        recv_sem=recv_sem,
        device_id={axis: peer},
        device_id_type=MESH,
    ).wait_recv()


def packed(rows):
    pieces = 16 // rows.shape[0]
    lanes = rows.shape[1] // pieces
    return jnp.concatenate(
        [rows[:, p * lanes : (p + 1) * lanes] for p in range(pieces)], axis=0
    ).astype(BF16)


def unpacked(tile, rows):
    tile = tile.astype(F32)
    return jnp.concatenate(
        [tile[p * rows : (p + 1) * rows] for p in range(tile.shape[0] // rows)], axis=1
    )


def half_rows(panel_ref, half, start):
    bands = panel_ref.shape[0] // 2
    pairs = [panel_ref[half * bands + k, :, pl.ds(start, BLOCK)] for k in range(bands)]
    return jnp.concatenate(
        [pair[0:1] for pair in pairs] + [pair[1:2] for pair in pairs], axis=0
    )


def all_rows(panel_ref, start):
    return jnp.concatenate([half_rows(panel_ref, half, start) for half in range(2)], axis=0)


def signed_index(index, length):
    return jnp.where(index < length // 2, index, index - length)


def fold_slab(slab_in, slab_rows, step, first):
    start = pl.multiple_of(step * BLOCK, BLOCK)
    tile = slab_in[:, :, pl.ds(pl.multiple_of((step - first) * BLOCK, BLOCK), BLOCK)]
    tile = tile.reshape(slab_rows.shape[0], BLOCK)
    slab_rows[:, pl.ds(start, BLOCK)] = tile
    return tile


def add_product(acc, slab_tile, pieces):
    right = jnp.concatenate(pieces, axis=0).astype(BF16)
    acc[...] += lax.dot_general(slab_tile, right, NT, preferred_element_type=F32)


def one_hot(size, places):
    grid = lax.broadcasted_iota(jnp.int32, (size, places.shape[1]), 0)
    return (grid == places).astype(F32).astype(BF16)


def first_kernel(
    sizes, wide, width, slot_ref, panel_ref, columns_ref, table_ref, slab_ref,
    out_ref, pos_ref, coef_ref, acc_ref, rows_ref,
    acc, picks, thirds, stage, land, pos_mine, pos_land, coef_land, slab_in, slab_rows,
    slab_sem, rows_sem, send_x, recv_x, send_c, recv_c, send_b, recv_b,
):
    n_one, n_two, length = sizes
    me, others = peers_of("pw")
    here, mates = peers_of("band")
    steps = slot_ref.shape[1] // BLOCK
    cols = acc.shape[1]
    side = land.shape[3] // 2
    size = 2 * panel_ref.shape[0]
    fetch = pltpu.make_async_copy(
        slab_ref.at[:, :, pl.ds(0, slab_in.shape[2])], slab_in, slab_sem
    )
    fetch.start()
    greet(("pw", "band"))

    def pack(step, carry):
        start = pl.multiple_of(step * BLOCK, BLOCK)
        coef_land[here, step] = packed(all_rows(panel_ref, start))
        return carry

    lax.fori_loop(0, steps, pack, 0)
    column = columns_ref[...]
    place_one = signed_index(column // n_two, n_one) + wide // 2
    place_two = signed_index(lax.rem(column, n_two), n_two) + wide // 2
    pos_mine[...] = place_two * wide + place_one
    pos_land[me] = pos_mine[...]
    copies = []
    for peer in others:
        copies.append(
            send_to("pw", peer, pos_mine, pos_land.at[me], send_c.at[peer], recv_c.at[me])
        )
    for mate in mates:
        copies.append(
            send_to(
                "band", mate, coef_land.at[here], coef_land.at[here], send_b.at[mate],
                recv_b.at[here],
            )
        )

    for half in range(2):
        acc[...] = jnp.zeros_like(acc)

        def scatter(step, carry):
            start = pl.multiple_of(step * BLOCK, BLOCK)
            if half == 0:
                slot = slot_ref[:, pl.ds(start, BLOCK)]
                third = lax.rem(lax.rem(slot, length) + width // 2, length)
                pick_col = one_hot(cols, slot // length)
                pick_third = one_hot(width, third)
                picks[step] = pick_col
                thirds[step] = pick_third
            else:
                pick_col = picks[step]
                pick_third = thirds[step]
            values = half_rows(panel_ref, half, start).astype(BF16)
            spread = jnp.concatenate(
                [pick_third * values[q : q + 1] for q in range(values.shape[0])], axis=0
            )
            acc[...] += lax.dot_general(spread, pick_col, NT, preferred_element_type=F32)
            return carry

        lax.fori_loop(0, steps, scatter, 0)
        got = acc[...].astype(BF16)
        done = lax.dot_general(got, table_ref[...], TN, preferred_element_type=F32)
        for d in range(land.shape[0]):
            piece = done[:, d * side : (d + 1) * side]
            stage[half, d] = jnp.concatenate(
                [piece[: cols // 2], piece[cols // 2 :]], axis=1
            ).astype(BF16)
        for peer in others:
            copies.append(
                send_to(
                    "pw", peer, stage.at[half, peer], land.at[me, half],
                    send_x.at[peer, half], recv_x.at[me, half],
                )
            )
        land[me, half] = stage[half, me]

    for mate in mates:
        arrived("band", mate, coef_land.at[mate], send_b.at[mate], recv_b.at[mate])
    fetch.wait()
    acc_ref[...] = jnp.zeros_like(acc_ref)

    def margin(step, carry):
        tile = fold_slab(slab_in, slab_rows, step, 0)
        add_product(
            acc_ref, tile, [unpacked(coef_land[b, step], size) for b in range(len(mates) + 1)]
        )
        return carry

    lax.fori_loop(0, slab_in.shape[2] // BLOCK, margin, 0)
    keep = pltpu.make_async_copy(slab_rows, rows_ref, rows_sem)
    keep.start()
    for peer in others:
        arrived("pw", peer, pos_land.at[peer], send_c.at[peer], recv_c.at[peer])
    pos_ref[...] = pos_land[...]
    coef_ref[...] = coef_land[...]
    for half in range(2):
        for peer in others:
            arrived(
                "pw", peer, land.at[peer, half], send_x.at[peer, half], recv_x.at[peer, half]
            )
    out_ref[...] = land[...]
    for copy in copies:
        copy.wait_send()
    keep.wait()


def first_part(slot, panel, columns, table, slab, sizes, wide, width, devices, mates):
    count, _, n = panel.shape
    cols = columns.shape[1]
    lanes = 2 * (table.shape[1] // devices)
    steps = n // BLOCK
    early = (steps // 2) * BLOCK
    rows = 2 * slab.shape[0]
    whole = pl.BlockSpec(memory_space=pltpu.VMEM)
    anywhere = pl.BlockSpec(memory_space=pl.ANY)
    coef_shape = (mates, steps, 16, BLOCK * count // 8)
    wave_shape = (devices, 2, cols // 2, lanes)
    dma = pltpu.SemaphoreType.DMA
    return pl.pallas_call(
        functools.partial(first_kernel, sizes, wide, width),
        in_specs=[whole] * 4 + [anywhere],
        out_specs=[whole] * 4 + [anywhere],
        out_shape=[
            jax.ShapeDtypeStruct(wave_shape, BF16),
            jax.ShapeDtypeStruct((devices, 1, cols), jnp.int32),
            jax.ShapeDtypeStruct(coef_shape, BF16),
            jax.ShapeDtypeStruct((rows, 2 * count * mates), F32),
            jax.ShapeDtypeStruct((rows, early), BF16),
        ],
        scratch_shapes=[
            pltpu.VMEM((count * width, cols), F32),
            pltpu.VMEM((steps, cols, BLOCK), BF16),
            pltpu.VMEM((steps, width, BLOCK), BF16),
            pltpu.VMEM((2, devices, cols // 2, lanes), BF16),
            pltpu.VMEM(wave_shape, BF16),
            pltpu.VMEM((1, cols), jnp.int32),
            pltpu.VMEM((devices, 1, cols), jnp.int32),
            pltpu.VMEM(coef_shape, BF16),
            pltpu.VMEM((slab.shape[0], 2, early), BF16),
            pltpu.VMEM((rows, early), BF16),
            dma,
            dma,
            dma((devices, 2)),
            dma((devices, 2)),
            dma((devices,)),
            dma((devices,)),
            dma((mates,)),
            dma((mates,)),
        ],
        compiler_params=pltpu.CompilerParams(
            vmem_limit_bytes=LIMIT, collective_id=1, has_side_effects=True
        ),
        name="first_part",
    )(slot, panel, columns, table, slab)


def plane_kernel(
    wide, n_one, n_two, pos_ref, x_ref, tx_ref, ty_ref, tyb_ref, txb_ref, v_ref, out_ref,
    wave, box, mid, mid_back,
):
    total, lanes = wave.shape
    planes = v_ref.shape[0] // n_one
    sign = jnp.where(
        lax.broadcasted_iota(jnp.int32, (1, lanes), 1) < lanes // 2, -1.0, 1.0
    ).astype(F32)
    devices, _, rows, _ = x_ref.shape
    piece = lanes // 4

    def quarters(tile):
        return [tile[:, p * piece : (p + 1) * piece] for p in range(4)]

    def unfold(d, carry):
        low = quarters(x_ref[d, 0].astype(F32))
        high = quarters(x_ref[d, 1].astype(F32))
        for side in range(2):
            base = pl.multiple_of((2 * d + side) * rows, rows)
            wave[pl.ds(base, rows), :] = jnp.concatenate(
                [low[2 * side], high[2 * side], low[2 * side + 1], high[2 * side + 1]], axis=1
            )
        return carry

    lax.fori_loop(0, devices, unfold, 0)
    box[...] = jnp.zeros_like(box)
    group = 16
    per = 2 * rows // group

    def put(step, carry):
        base = pl.multiple_of(step * group, group)
        tile = wave[pl.ds(base, group), :]
        d = step // per
        start = (step - d * per) * group
        for u in range(group):
            box[pl.ds(pos_ref[d, 0, start + u], 1), :] = tile[u : u + 1]
        return carry

    lax.fori_loop(0, total // group, put, 0)

    def stacked(tiles):
        plain = jnp.concatenate(tiles, axis=1)
        turned = jnp.concatenate(
            [pltpu.roll(tile, lanes // 2, 1) * sign for tile in tiles], axis=1
        )
        return jnp.concatenate([plain, turned], axis=0).astype(BF16)

    def split(got):
        return [got[:, u * lanes : (u + 1) * lanes] for u in range(got.shape[1] // lanes)]

    def inverse_one(step, carry):
        tiles = [box[pl.ds(pl.multiple_of((2 * step + u) * wide, 8), wide), :] for u in range(2)]
        got = jnp.dot(tx_ref[...], stacked(tiles), preferred_element_type=F32)
        for u, tile in enumerate(split(got)):
            mid[pl.ds(2 * step + u, n_one, stride=wide), :] = tile
        return carry

    lax.fori_loop(0, wide // 2, inverse_one, 0, unroll=4)

    def both_two(step, carry):
        starts = [pl.multiple_of((2 * step + u) * wide, 8) for u in range(2)]
        tiles = [mid[pl.ds(start, wide), :] for start in starts]
        got = jnp.dot(ty_ref[...], stacked(tiles), preferred_element_type=F32)
        tiles = []
        for u, tile in enumerate(split(got)):
            local = v_ref[pl.ds(2 * step + u, planes, stride=n_one), :]
            tiles.append(tile * jnp.concatenate([local] * (lanes // planes), axis=0).T)
        back = jnp.dot(tyb_ref[...], stacked(tiles), preferred_element_type=F32)
        for u, tile in enumerate(split(back)):
            mid_back[pl.ds(starts[u], wide), :] = tile
        return carry

    lax.fori_loop(0, n_one // 2, both_two, 0, unroll=4)

    def forward_one(step, carry):
        tiles = [mid_back[pl.ds(2 * step + u, n_one, stride=wide), :] for u in range(2)]
        got = jnp.dot(txb_ref[...], stacked(tiles), preferred_element_type=F32)
        for u, tile in enumerate(split(got)):
            start = pl.multiple_of((2 * step + u) * wide, 8)
            box[pl.ds(start, wide), :] = tile
        return carry

    lax.fori_loop(0, wide // 2, forward_one, 0, unroll=4)

    def take(step, carry):
        base = pl.multiple_of(step * group, group)
        d = step // per
        start = (step - d * per) * group
        taken = [box[pl.ds(pos_ref[d, 0, start + u], 1), :] for u in range(group)]
        for u in range(group):
            wave[pl.ds(base + u, 1), :] = taken[u]
        return carry

    lax.fori_loop(0, total // group, take, 0)

    def fold(d, carry):
        sides = [
            quarters(wave[pl.ds(pl.multiple_of((2 * d + side) * rows, rows), rows), :])
            for side in range(2)
        ]
        for half in range(2):
            out_ref[d, half] = jnp.concatenate(
                [sides[side][half + 2 * which] for side in range(2) for which in range(2)], axis=1
            ).astype(BF16)
        return carry

    lax.fori_loop(0, devices, fold, 0)


def plane_part(pos, x, tables, potential_rows, wide, n_one, n_two):
    devices, _, rows, lanes = x.shape
    total = 2 * devices * rows
    whole = pl.BlockSpec(memory_space=pltpu.VMEM)
    return pl.pallas_call(
        functools.partial(plane_kernel, wide, n_one, n_two),
        in_specs=[pl.BlockSpec(memory_space=pltpu.SMEM)] + [whole] * 6,
        out_specs=whole,
        out_shape=jax.ShapeDtypeStruct(x.shape, BF16),
        scratch_shapes=[
            pltpu.VMEM((total, lanes), F32),
            pltpu.VMEM((wide * wide, lanes), F32),
            pltpu.VMEM((n_one * wide, lanes), F32),
            pltpu.VMEM((n_one * wide, lanes), F32),
        ],
        compiler_params=pltpu.CompilerParams(vmem_limit_bytes=LIMIT),
        name="plane_part",
    )(pos, x, *tables, potential_rows)


def last_kernel(
    sizes, width, groups, slot_ref, panel_ref, columns_ref, x_ref, table_ref, coef_ref, acc_ref,
    rows_ref, slab_ref, out_ref,
    home, held, picks, kinetics, app, slab_in, slab_rows, acc_h, acc_m, terms, part, parts,
    slab_sem, rows_sem, send_x, recv_x, send_b, recv_b, send_p, recv_p,
):
    n_one, n_two, length = sizes
    me, others = peers_of("pw")
    here, mates = peers_of("band")
    bands = len(mates) + 1
    count = panel_ref.shape[0]
    size = 2 * count
    body = count * width
    cols = held.shape[1]
    steps = slot_ref.shape[1] // BLOCK
    each = steps // groups
    early = rows_ref.shape[1]
    fetch = pltpu.make_async_copy(
        slab_ref.at[:, :, pl.ds(early, slab_in.shape[2])], slab_in, slab_sem
    )
    fetch.start()
    again = pltpu.make_async_copy(rows_ref, slab_rows.at[:, pl.ds(0, early)], rows_sem)
    again.start()
    greet(("pw", "band"))
    copies = []
    for half in range(2):
        for peer in others:
            copies.append(
                send_to(
                    "pw", peer, x_ref.at[peer, half], home.at[me, half],
                    send_x.at[peer, half], recv_x.at[me, half],
                )
            )
    home[me] = x_ref[me]
    column = columns_ref[...]
    held[body:, :] = jnp.concatenate(
        [
            signed_index(column // n_two, n_one),
            signed_index(lax.rem(column, n_two), n_two),
            jnp.zeros((14, cols), jnp.int32),
        ],
        axis=0,
    ).astype(F32).astype(BF16)
    acc_h[...] = jnp.zeros_like(acc_h)
    acc_m[...] = acc_ref[...]
    fetch.wait()

    def margin(step, carry):
        tile = fold_slab(slab_in, slab_rows, step, early // BLOCK)
        add_product(acc_m, tile, [unpacked(coef_ref[b, step], size) for b in range(bands)])
        return carry

    lax.fori_loop(early // BLOCK, steps, margin, 0)
    again.wait()

    for half in range(2):
        for peer in others:
            arrived(
                "pw", peer, home.at[peer, half], send_x.at[peer, half], recv_x.at[peer, half]
            )
        pieces = [home[d, half].astype(F32) for d in range(home.shape[0])]
        side = home.shape[3] // 2
        x = jnp.concatenate(
            [
                jnp.concatenate([piece[:, :side] for piece in pieces], axis=1),
                jnp.concatenate([piece[:, side:] for piece in pieces], axis=1),
            ],
            axis=0,
        ).astype(BF16)
        held[:body, :] = lax.dot_general(
            table_ref[...], x, NT, preferred_element_type=F32
        ).astype(BF16)

        def gather(step, carry):
            start = pl.multiple_of(step * BLOCK, BLOCK)
            slot = slot_ref[:, pl.ds(start, BLOCK)]
            third = lax.rem(slot, length)
            place = lax.rem(third + width // 2, length)
            at_third = lax.broadcasted_iota(jnp.int32, (width, BLOCK), 0) == place
            if half == 0:
                pick_col = one_hot(cols, slot // length)
                picks[step] = pick_col
                got = jnp.dot(held[...], pick_col, preferred_element_type=F32)
                f_one = got[body : body + 1] * (2.0 / n_one)
                f_two = got[body + 1 : body + 2] * (2.0 / n_two)
                f_three = signed_index(third, length).astype(F32) * (2.0 / length)
                kinetic = 0.5 * (f_one * f_one + f_two * f_two + f_three * f_three)
                kinetics[:, pl.ds(start, BLOCK)] = kinetic
            else:
                got = jnp.dot(held[:body, :], picks[step], preferred_element_type=F32)
                kinetic = kinetics[:, pl.ds(start, BLOCK)]
            picked = jnp.concatenate(
                [
                    jnp.sum(
                        jnp.where(at_third, got[q * width : (q + 1) * width], 0.0),
                        axis=0,
                        keepdims=True,
                    )
                    for q in range(count)
                ],
                axis=0,
            )
            app[here, half, step] = packed(kinetic * half_rows(panel_ref, half, start) + picked)
            return carry

        for g in range(groups):
            lax.fori_loop(g * each, (g + 1) * each, gather, 0)
            span = pl.ds(g * each, each)
            for mate in mates:
                copies.append(
                    send_to(
                        "band", mate, app.at[here, half, span], app.at[here, half, span],
                        send_b.at[mate, half, g], recv_b.at[here, half, g],
                    )
                )

    def hamiltonian(step, carry):
        start = pl.multiple_of(step * BLOCK, BLOCK)
        add_product(
            acc_h,
            slab_rows[:, pl.ds(start, BLOCK)],
            [unpacked(app[b, half, step], count) for b in range(bands) for half in range(2)],
        )
        return carry

    for g in range(groups):
        span = pl.ds(g * each, each)
        for mate in mates:
            for half in range(2):
                arrived(
                    "band", mate, app.at[mate, half, span], send_b.at[mate, half, g],
                    recv_b.at[mate, half, g],
                )
        lax.fori_loop(g * each, (g + 1) * each, hamiltonian, 0)

    terms[...] = jnp.concatenate([acc_h[...], acc_m[...]], axis=1)
    rows = terms.shape[0] // 2
    real_rows = terms[pl.ds(0, rows, stride=2), :].T
    imag_rows = terms[pl.ds(1, rows, stride=2), :].T

    def pick(value, kind, which):
        first = kind * bands * size + which * (count // 2)
        return jnp.concatenate(
            [value[first + b * count : first + b * count + count // 2] for b in range(2 * bands)],
            axis=0,
        )

    pieces = []
    for kind in range(2):
        pieces.append(pick(real_rows, kind, 0) + pick(imag_rows, kind, 1))
        pieces.append(pick(real_rows, kind, 1) - pick(imag_rows, kind, 0))
    part[...] = jnp.concatenate(pieces, axis=0)
    share = out_ref.shape[0]

    def block_of(index):
        return pl.ds(pl.multiple_of(index * share, share), share)

    for peer in others:
        copies.append(
            send_to(
                "pw", peer, part.at[block_of(peer)], parts.at[me], send_p.at[peer], recv_p.at[me]
            )
        )
    parts[me] = part[block_of(me), :]
    for peer in others:
        arrived("pw", peer, parts.at[peer], send_p.at[peer], recv_p.at[peer])
    total = parts[0]
    for d in range(1, parts.shape[0]):
        total = total + parts[d]
    out_ref[...] = total
    for copy in copies:
        copy.wait_send()


def last_part(slot, panel, columns, x, table, coef, margin, slab_rows, slab, sizes, width):
    devices = x.shape[0]
    cols = columns.shape[1]
    count, _, n = panel.shape
    mates, steps = coef.shape[:2]
    size = 2 * count
    rows = slab.shape[0]
    groups = 3 if steps % 3 == 0 else 1
    share = 2 * mates * size // devices
    whole = pl.BlockSpec(memory_space=pltpu.VMEM)
    anywhere = pl.BlockSpec(memory_space=pl.ANY)
    dma = pltpu.SemaphoreType.DMA
    return pl.pallas_call(
        functools.partial(last_kernel, sizes, width, groups),
        in_specs=[whole] * 7 + [anywhere] * 2,
        out_specs=whole,
        out_shape=jax.ShapeDtypeStruct((share, rows), F32),
        scratch_shapes=[
            pltpu.VMEM(x.shape, BF16),
            pltpu.VMEM((count * width + 16, cols), BF16),
            pltpu.VMEM((steps, cols, BLOCK), BF16),
            pltpu.VMEM((1, n), F32),
            pltpu.VMEM((mates, 2, steps, 16, BLOCK * count // 16), BF16),
            pltpu.VMEM((rows, 2, n - slab_rows.shape[1]), BF16),
            pltpu.VMEM((2 * rows, n), BF16),
            pltpu.VMEM((2 * rows, mates * size), F32),
            pltpu.VMEM((2 * rows, mates * size), F32),
            pltpu.VMEM((2 * rows, 2 * mates * size), F32),
            pltpu.VMEM((2 * mates * size, rows), F32),
            pltpu.VMEM((devices, share, rows), F32),
            dma,
            dma,
            dma((devices, 2)),
            dma((devices, 2)),
            dma((mates, 2, groups)),
            dma((mates, 2, groups)),
            dma((devices,)),
            dma((devices,)),
        ],
        compiler_params=pltpu.CompilerParams(
            vmem_limit_bytes=LIMIT, collective_id=2, has_side_effects=True
        ),
        name="last_part",
    )(slot, panel, columns, x, table, coef, margin, slab_rows, slab)


def per_device(slab, panel, potential, pw_slot, columns):
    devices = lax.axis_size("pw")
    mates = lax.axis_size("band")
    planes, n_one, n_two = potential.shape
    length = planes * devices
    cols = columns.shape[0]
    count = panel.shape[0]
    n = panel.shape[2]

    square = disk_square(n_one, n_two, cols * devices)
    wide = odd_tiles(window(math.isqrt(square), 8, max(n_one, n_two)))
    reach = math.isqrt(square + (-(-n // (2 * cols)) + 2) ** 2) + 1
    width = window(reach, 16, length)

    ztab = jnp.asarray(z_tables(count // 2, length, planes, width), BF16)
    cy, sy = cos_sin(np.arange(n_two), signed_of(wide), n_two)
    cx, sx = cos_sin(np.arange(n_one), signed_of(wide), n_one)
    tables = [
        np.concatenate([cx, sx], axis=1),
        np.concatenate([cy, sy], axis=1),
        np.concatenate([cy.T, -sy.T], axis=1),
        np.concatenate([cx.T, -sx.T], axis=1),
    ]
    tables = [jnp.asarray(t, BF16) for t in tables]

    slot = pw_slot.reshape(1, n)
    owned = columns.reshape(1, cols)
    sizes = (n_one, n_two, length)
    there, pos, coef, margin, slab_rows = first_part(
        slot, panel, owned, ztab, slab, sizes, wide, width, devices, mates
    )
    worked = plane_part(
        pos, there, tables, potential.reshape(planes * n_one, n_two), wide, n_one, n_two
    )
    out = last_part(
        slot, panel, owned, worked, ztab, coef, margin, slab_rows, slab, sizes, width
    )
    return out.T


def solution(mesh):
    in_specs = (P("band", None, "pw"), P("band", None, "pw"), P("pw", None, None), P("pw"), P("pw"))
    out_specs = P("band", "pw")
    return jax.shard_map(
        per_device, mesh=mesh, in_specs=in_specs, out_specs=out_specs, check_vma=False
    )
```

time: 89.7 us -> 91.2 us (1.017)
  Pallas kernels: 85.4 us -> 89.7 us
  other arithmetic: 2.66 us -> 0 us
    pallas_call x1, Pallas kernels: 20.8 us -> 29.7 us  [plane_part(): pl.pallas_call(functools.partial(plane_kernel, wide, n_one, n_two), in_sp...]
    pallas_call x2, Pallas kernels: 64.6 us -> 60 us  [the longest x1 34.1 us: last_part(): pl.pallas_call(functools.partial(last_kernel, sizes, width, groups), in_s...]
    add x1 -> x0, other arithmetic: 1.3 us -> none  [per_device(): place_two * wide + place_one]
where the time goes in v2:
time: 91.2 us; the launch traced here: 90.9 us
  Pallas kernels  89.7 us (98%)
  local copies, waits for them, and re-layouts  1.27 us (1%)
    pallas_call x1, Pallas kernels, last_part(): pl.pallas_call(functools.partial(last_kernel, sizes, width, groups), in_s...  34.1 us
    pallas_call x1, Pallas kernels, plane_part(): pl.pallas_call(functools.partial(plane_kernel, wide, n_one, n_two), in_sp...  29.7 us
    pallas_call x1, Pallas kernels, first_part(): pl.pallas_call(functools.partial(first_kernel, sizes, wide, width), in_sp...  25.9 us

profile of v2, /device:TPU:0, one launch (start us, length us, event | category | flops | bytes accessed | tf_op | source)
XLA Modules:
  0.0 90.9 jit_solution(4019623754417795677)
XLA Ops:
  0.0 25.9 %first_part.1 = (bf16[8,2,128,128]{3,2,1,0:T(8,128)(2,1)}, s32[8,1,256]{2,1,0:T(1,128)}, bf16[4,12,16,512]{3,2,1,0:T(8,128)(2,1)}, f32[256,32]{1,0:T(8,128)}, bf16[256,6144]{1,0:T(8,128)(2,1)}) custom-call(s32[1,12288]{1,0:T(1,128)} %bitcast.5, f32[4,2,12288]{2,1,0:T(2,128)} %panel_ref.3, s32[1,256]{1,0:T(1,128)} %bitcast.8, ...), custom_call_target="tpu_custom_call" | custom-call | tf_op jit(solution)/shard_map/first_part/pallas_call | solution.py:278
  25.9 29.7 %plane_part.1.x_ref = bf16[8,2,128,128]{3,2,1,0:T(8,128)(2,1)} custom-call(s32[8,1,256]{2,1,0:T(1,128)} %get-tuple-element.10.pos_ref, bf16[8,2,128,128]{3,2,1,0:T(8,128)(2,1)} %get-tuple-element.11.x_ref, bf16[128,112]{1,0:T(8,128)(2,1)} %constant.7.clone.tx_ref.ty_ref, bf16[128,112]{1,0:T(8,128)(2,1)} %constant.7.clone.tx_ref.ty_ref, ...), custom_call_target="tpu_custom_call" | custom-call | tf_op jit(solution)/shard_map/plane_part/pallas_call | solution.py:430
  55.6 34.1 %last_part.1 = f32[8,128]{1,0:T(8,128)} custom-call(s32[1,12288]{1,0:T(1,128)} %bitcast.6, f32[4,2,12288]{2,1,0:T(2,128)} %panel_ref.3, s32[1,256]{1,0:T(1,128)} %bitcast.9, bf16[8,2,128,128]{3,2,1,0:T(8,128)(2,1)} %plane_part.1.x_ref, bf16[320,512]{1,0:T(8,128)(2,1)} %constant.6.clone.table_ref, bf16[4,12,16,512]{3,2,1,0:T(8,128)(2,1)} %get-tuple-element.12.coef_ref, ...), custom_call_target="tpu_custom_call" | custom-call | tf_op jit(solution)/shard_map/last_part/pallas_call | solution.py:632
  89.7 1.3 %copy.12 = f32[128,8]{0,1:T(8,128)} copy(f32[128,8]{0,1:T(8,128)} %bitcast.7) | data formatting | bytes 8192

commit v3 on v2

--- a/solution.py
+++ b/solution.py
@@ -133,17 +133,42 @@
     return jnp.where(index < length // 2, index, index - length)
 
 
-def fold_slab(slab_in, slab_rows, step, first):
-    start = pl.multiple_of(step * BLOCK, BLOCK)
-    tile = slab_in[:, :, pl.ds(pl.multiple_of((step - first) * BLOCK, BLOCK), BLOCK)]
-    tile = tile.reshape(slab_rows.shape[0], BLOCK)
-    slab_rows[:, pl.ds(start, BLOCK)] = tile
-    return tile
-
-
-def add_product(acc, slab_tile, pieces):
-    right = jnp.concatenate(pieces, axis=0).astype(BF16)
-    acc[...] += lax.dot_general(slab_tile, right, NT, preferred_element_type=F32)
+def add_products(acc, slab_in, step, rows_of):
+    tiles = BLOCK // 128
+    deep = 2 * tiles
+    rights = []
+    for u in range(2):
+        right = jnp.concatenate(rows_of(2 * step + u), axis=0).astype(BF16)
+        rights.append(
+            jnp.concatenate([right[:, t * 128 : (t + 1) * 128] for t in range(tiles)], axis=0)
+        )
+    right = jnp.concatenate(rights, axis=1)
+    some = 32
+    first = pl.multiple_of(2 * step * deep, 2 * deep)
+    for j in range(0, slab_in.shape[0], some):
+        left = jnp.concatenate(
+            [
+                slab_in[pl.ds(j, some), pl.ds(first + u * deep, deep), :].reshape(some * deep, 128)
+                for u in range(2)
+            ],
+            axis=1,
+        )
+        got = lax.dot_general(left, right, NT, preferred_element_type=F32)
+        for tile in range(acc.shape[0]):
+            acc[tile, pl.ds(j * deep, some * deep), :] += got[:, tile * 128 : (tile + 1) * 128]
+
+
+def collapse(acc, part, width):
+    tiles = BLOCK // 128
+    deep = 2 * tiles
+    rows = acc.shape[1] // deep
+    total = None
+    for t in range(tiles):
+        lane = t * width
+        piece = acc[lane // 128, pl.ds(2 * t + part, rows, stride=deep), :]
+        piece = piece[:, lane % 128 : lane % 128 + width]
+        total = piece if total is None else total + piece
+    return total
 
 
 def one_hot(size, places):
@@ -153,9 +178,9 @@
 
 def first_kernel(
     sizes, wide, width, slot_ref, panel_ref, columns_ref, table_ref, slab_ref,
-    out_ref, pos_ref, coef_ref, acc_ref, rows_ref,
-    acc, picks, thirds, stage, land, pos_mine, pos_land, coef_land, slab_in, slab_rows,
-    slab_sem, rows_sem, send_x, recv_x, send_c, recv_c, send_b, recv_b,
+    out_ref, pos_ref, margin_ref,
+    acc, picks, thirds, stage, land, pos_mine, pos_land, coef_land, slab_in, acc_m,
+    slab_sem, send_x, recv_x, send_c, recv_c, send_b, recv_b,
 ):
     n_one, n_two, length = sizes
     me, others = peers_of("pw")
@@ -164,9 +189,7 @@
     cols = acc.shape[1]
     side = land.shape[3] // 2
     size = 2 * panel_ref.shape[0]
-    fetch = pltpu.make_async_copy(
-        slab_ref.at[:, :, pl.ds(0, slab_in.shape[2])], slab_in, slab_sem
-    )
+    fetch = pltpu.make_async_copy(slab_ref, slab_in, slab_sem)
     fetch.start()
     greet(("pw", "band"))
 
@@ -236,22 +259,23 @@
     for mate in mates:
         arrived("band", mate, coef_land.at[mate], send_b.at[mate], recv_b.at[mate])
     fetch.wait()
-    acc_ref[...] = jnp.zeros_like(acc_ref)
+    acc_m[...] = jnp.zeros_like(acc_m)
 
     def margin(step, carry):
-        tile = fold_slab(slab_in, slab_rows, step, 0)
-        add_product(
-            acc_ref, tile, [unpacked(coef_land[b, step], size) for b in range(len(mates) + 1)]
-        )
-        return carry
-
-    lax.fori_loop(0, slab_in.shape[2] // BLOCK, margin, 0)
-    keep = pltpu.make_async_copy(slab_rows, rows_ref, rows_sem)
-    keep.start()
+        add_products(
+            acc_m,
+            slab_in,
+            step,
+            lambda block: [unpacked(coef_land[b, block], size) for b in range(len(mates) + 1)],
+        )
+        return carry
+
+    lax.fori_loop(0, steps // 2, margin, 0)
+    for which in range(2):
+        margin_ref[which] = collapse(acc_m, which, margin_ref.shape[2])
     for peer in others:
         arrived("pw", peer, pos_land.at[peer], send_c.at[peer], recv_c.at[peer])
     pos_ref[...] = pos_land[...]
-    coef_ref[...] = coef_land[...]
     for half in range(2):
         for peer in others:
             arrived(
@@ -260,7 +284,6 @@
     out_ref[...] = land[...]
     for copy in copies:
         copy.wait_send()
-    keep.wait()
 
 
 def first_part(slot, panel, columns, table, slab, sizes, wide, width, devices, mates):
@@ -268,8 +291,8 @@
     cols = columns.shape[1]
     lanes = 2 * (table.shape[1] // devices)
     steps = n // BLOCK
-    early = (steps // 2) * BLOCK
-    rows = 2 * slab.shape[0]
+    rows = slab.shape[0]
+    pair = 2 * count * mates
     whole = pl.BlockSpec(memory_space=pltpu.VMEM)
     anywhere = pl.BlockSpec(memory_space=pl.ANY)
     coef_shape = (mates, steps, 16, BLOCK * count // 8)
@@ -278,13 +301,11 @@
     return pl.pallas_call(
         functools.partial(first_kernel, sizes, wide, width),
         in_specs=[whole] * 4 + [anywhere],
-        out_specs=[whole] * 4 + [anywhere],
+        out_specs=[whole] * 3,
         out_shape=[
             jax.ShapeDtypeStruct(wave_shape, BF16),
             jax.ShapeDtypeStruct((devices, 1, cols), jnp.int32),
-            jax.ShapeDtypeStruct(coef_shape, BF16),
-            jax.ShapeDtypeStruct((rows, 2 * count * mates), F32),
-            jax.ShapeDtypeStruct((rows, early), BF16),
+            jax.ShapeDtypeStruct((2, rows, pair), F32),
         ],
         scratch_shapes=[
             pltpu.VMEM((count * width, cols), F32),
@@ -295,9 +316,8 @@
             pltpu.VMEM((1, cols), jnp.int32),
             pltpu.VMEM((devices, 1, cols), jnp.int32),
             pltpu.VMEM(coef_shape, BF16),
-            pltpu.VMEM((slab.shape[0], 2, early), BF16),
-            pltpu.VMEM((rows, early), BF16),
-            dma,
+            pltpu.VMEM(slab.shape, BF16),
+            pltpu.VMEM((pair * BLOCK // 128 // 128, rows * BLOCK // 64, 128), F32),
             dma,
             dma((devices, 2)),
             dma((devices, 2)),
@@ -341,15 +361,12 @@
     lax.fori_loop(0, devices, unfold, 0)
     box[...] = jnp.zeros_like(box)
     group = 16
-    per = 2 * rows // group
 
     def put(step, carry):
         base = pl.multiple_of(step * group, group)
         tile = wave[pl.ds(base, group), :]
-        d = step // per
-        start = (step - d * per) * group
         for u in range(group):
-            box[pl.ds(pos_ref[d, 0, start + u], 1), :] = tile[u : u + 1]
+            box[pl.ds(pos_ref[base + u], 1), :] = tile[u : u + 1]
         return carry
 
     lax.fori_loop(0, total // group, put, 0)
@@ -400,9 +417,7 @@
 
     def take(step, carry):
         base = pl.multiple_of(step * group, group)
-        d = step // per
-        start = (step - d * per) * group
-        taken = [box[pl.ds(pos_ref[d, 0, start + u], 1), :] for u in range(group)]
+        taken = [box[pl.ds(pos_ref[base + u], 1), :] for u in range(group)]
         for u in range(group):
             wave[pl.ds(base + u, 1), :] = taken[u]
         return carry
@@ -444,10 +459,10 @@
 
 
 def last_kernel(
-    sizes, width, groups, slot_ref, panel_ref, columns_ref, x_ref, table_ref, coef_ref, acc_ref,
-    rows_ref, slab_ref, out_ref,
-    home, held, picks, kinetics, app, slab_in, slab_rows, acc_h, acc_m, terms, part, parts,
-    slab_sem, rows_sem, send_x, recv_x, send_b, recv_b, send_p, recv_p,
+    sizes, width, groups, slot_ref, panel_ref, columns_ref, x_ref, table_ref, margin_ref,
+    slab_ref, out_ref,
+    home, held, picks, kinetics, app, slab_in, acc_h, part, parts,
+    slab_sem, send_x, recv_x, send_b, recv_b, send_p, recv_p,
 ):
     n_one, n_two, length = sizes
     me, others = peers_of("pw")
@@ -459,13 +474,8 @@
     cols = held.shape[1]
     steps = slot_ref.shape[1] // BLOCK
     each = steps // groups
-    early = rows_ref.shape[1]
-    fetch = pltpu.make_async_copy(
-        slab_ref.at[:, :, pl.ds(early, slab_in.shape[2])], slab_in, slab_sem
-    )
+    fetch = pltpu.make_async_copy(slab_ref, slab_in, slab_sem)
     fetch.start()
-    again = pltpu.make_async_copy(rows_ref, slab_rows.at[:, pl.ds(0, early)], rows_sem)
-    again.start()
     greet(("pw", "band"))
     copies = []
     for half in range(2):
@@ -487,16 +497,7 @@
         axis=0,
     ).astype(F32).astype(BF16)
     acc_h[...] = jnp.zeros_like(acc_h)
-    acc_m[...] = acc_ref[...]
     fetch.wait()
-
-    def margin(step, carry):
-        tile = fold_slab(slab_in, slab_rows, step, early // BLOCK)
-        add_product(acc_m, tile, [unpacked(coef_ref[b, step], size) for b in range(bands)])
-        return carry
-
-    lax.fori_loop(early // BLOCK, steps, margin, 0)
-    again.wait()
 
     for half in range(2):
         for peer in others:
@@ -560,11 +561,13 @@
                 )
 
     def hamiltonian(step, carry):
-        start = pl.multiple_of(step * BLOCK, BLOCK)
-        add_product(
+        add_products(
             acc_h,
-            slab_rows[:, pl.ds(start, BLOCK)],
-            [unpacked(app[b, half, step], count) for b in range(bands) for half in range(2)],
+            slab_in,
+            step,
+            lambda block: [
+                unpacked(app[b, half, block], count) for b in range(bands) for half in range(2)
+            ],
         )
         return carry
 
@@ -576,12 +579,13 @@
                     "band", mate, app.at[mate, half, span], send_b.at[mate, half, g],
                     recv_b.at[mate, half, g],
                 )
-        lax.fori_loop(g * each, (g + 1) * each, hamiltonian, 0)
-
-    terms[...] = jnp.concatenate([acc_h[...], acc_m[...]], axis=1)
-    rows = terms.shape[0] // 2
-    real_rows = terms[pl.ds(0, rows, stride=2), :].T
-    imag_rows = terms[pl.ds(1, rows, stride=2), :].T
+        lax.fori_loop(g * each // 2, (g + 1) * each // 2, hamiltonian, 0)
+
+    width_h = margin_ref.shape[2]
+    real_rows, imag_rows = [
+        jnp.concatenate([collapse(acc_h, which, width_h), margin_ref[which]], axis=1).T
+        for which in range(2)
+    ]
 
     def pick(value, kind, which):
         first = kind * bands * size + which * (count // 2)
@@ -617,21 +621,21 @@
         copy.wait_send()
 
 
-def last_part(slot, panel, columns, x, table, coef, margin, slab_rows, slab, sizes, width):
+def last_part(slot, panel, columns, x, table, margin, slab, sizes, width, mates):
     devices = x.shape[0]
     cols = columns.shape[1]
     count, _, n = panel.shape
-    mates, steps = coef.shape[:2]
+    steps = n // BLOCK
     size = 2 * count
     rows = slab.shape[0]
-    groups = 3 if steps % 3 == 0 else 1
+    groups = 3 if steps % 6 == 0 else 1
     share = 2 * mates * size // devices
     whole = pl.BlockSpec(memory_space=pltpu.VMEM)
     anywhere = pl.BlockSpec(memory_space=pl.ANY)
     dma = pltpu.SemaphoreType.DMA
     return pl.pallas_call(
         functools.partial(last_kernel, sizes, width, groups),
-        in_specs=[whole] * 7 + [anywhere] * 2,
+        in_specs=[whole] * 6 + [anywhere],
         out_specs=whole,
         out_shape=jax.ShapeDtypeStruct((share, rows), F32),
         scratch_shapes=[
@@ -640,14 +644,10 @@
             pltpu.VMEM((steps, cols, BLOCK), BF16),
             pltpu.VMEM((1, n), F32),
             pltpu.VMEM((mates, 2, steps, 16, BLOCK * count // 16), BF16),
-            pltpu.VMEM((rows, 2, n - slab_rows.shape[1]), BF16),
-            pltpu.VMEM((2 * rows, n), BF16),
-            pltpu.VMEM((2 * rows, mates * size), F32),
-            pltpu.VMEM((2 * rows, mates * size), F32),
-            pltpu.VMEM((2 * rows, 2 * mates * size), F32),
+            pltpu.VMEM(slab.shape, BF16),
+            pltpu.VMEM((mates * size * BLOCK // 128 // 128, rows * BLOCK // 64, 128), F32),
             pltpu.VMEM((2 * mates * size, rows), F32),
             pltpu.VMEM((devices, share, rows), F32),
-            dma,
             dma,
             dma((devices, 2)),
             dma((devices, 2)),
@@ -660,7 +660,7 @@
             vmem_limit_bytes=LIMIT, collective_id=2, has_side_effects=True
         ),
         name="last_part",
-    )(slot, panel, columns, x, table, coef, margin, slab_rows, slab)
+    )(slot, panel, columns, x, table, margin, slab)
 
 
 def per_device(slab, panel, potential, pw_slot, columns):
@@ -691,14 +691,16 @@
     slot = pw_slot.reshape(1, n)
     owned = columns.reshape(1, cols)
     sizes = (n_one, n_two, length)
-    there, pos, coef, margin, slab_rows = first_part(
+    slab = slab.reshape(slab.shape[0], 2, n // 128, 128)
+    slab = slab.transpose(0, 2, 1, 3).reshape(slab.shape[0], n // 64, 128)
+    there, pos, margin = first_part(
         slot, panel, owned, ztab, slab, sizes, wide, width, devices, mates
     )
     worked = plane_part(
-        pos, there, tables, potential.reshape(planes * n_one, n_two), wide, n_one, n_two
+        pos.reshape(devices * cols), there, tables, potential.reshape(planes * n_one, n_two), wide, n_one, n_two
     )
     out = last_part(
-        slot, panel, owned, worked, ztab, coef, margin, slab_rows, slab, sizes, width
+        slot, panel, owned, worked, ztab, margin, slab, sizes, width, mates
     )
     return out.T
 

time: 91.2 us -> 83.5 us (0.916)
  Pallas kernels: 89.7 us -> 82 us
    pallas_call x1, Pallas kernels: 29.7 us -> 22.5 us  [plane_part(): pl.pallas_call(functools.partial(plane_kernel, wide, n_one, n_two), in_sp...]
where the time goes in v3:
time: 83.5 us; the launch traced here: 83.3 us
  Pallas kernels  82 us (98%)
  local copies, waits for them, and re-layouts  1.27 us (2%)
    pallas_call x1, Pallas kernels, last_part(): pl.pallas_call(functools.partial(last_kernel, sizes, width, groups), in_s...  33.9 us
    pallas_call x1, Pallas kernels, first_part(): pl.pallas_call(functools.partial(first_kernel, sizes, wide, width), in_sp...  25.6 us
    pallas_call x1, Pallas kernels, plane_part(): pl.pallas_call(functools.partial(plane_kernel, wide, n_one, n_two), in_sp...  22.5 us

profile of v3, /device:TPU:0, one launch (start us, length us, event | category | flops | bytes accessed | tf_op | source)
XLA Modules:
  0.0 83.3 jit_solution(4412804120375881831)
XLA Ops:
  0.0 25.6 %first_part.1 = (bf16[8,2,128,128]{3,2,1,0:T(8,128)(2,1)}, s32[8,1,256]{2,1,0:T(1,128)}, f32[2,128,32]{2,1,0:T(8,128)}) custom-call(s32[1,12288]{1,0:T(1,128)} %bitcast.13, f32[4,2,12288]{2,1,0:T(2,128)} %panel_ref.3, s32[1,256]{1,0:T(1,128)} %bitcast.17, bf16[320,512]{1,0:T(8,128)(2,1)} %constant.6.clone.table_ref, bf16[128,192,128]{2,1,0:T(8,128)(2,1)} %bitcast.10), custom_call_target="tpu_custom_call" | custom-call | tf_op jit(solution)/shard_map/first_part/pallas_call | solution.py:301
  25.6 22.5 %plane_part.1.x_ref = bf16[8,2,128,128]{3,2,1,0:T(8,128)(2,1)} custom-call(s32[2048]{0:T(1024)} %bitcast.16, bf16[8,2,128,128]{3,2,1,0:T(8,128)(2,1)} %get-tuple-element.9.x_ref, bf16[128,112]{1,0:T(8,128)(2,1)} %constant.7.clone.tx_ref.ty_ref, bf16[128,112]{1,0:T(8,128)(2,1)} %constant.7.clone.tx_ref.ty_ref, bf16[56,256]{1,0:T(8,128)(2,1)} %constant.8.clone.tyb_ref.txb_ref, ...), custom_call_target="tpu_custom_call" | custom-call | tf_op jit(solution)/shard_map/plane_part/pallas_call | solution.py:445
  48.1 33.9 %last_part.1 = f32[8,128]{1,0:T(8,128)} custom-call(s32[1,12288]{1,0:T(1,128)} %bitcast.14, f32[4,2,12288]{2,1,0:T(2,128)} %panel_ref.3, s32[1,256]{1,0:T(1,128)} %bitcast.18, bf16[8,2,128,128]{3,2,1,0:T(8,128)(2,1)} %plane_part.1.x_ref, bf16[320,512]{1,0:T(8,128)(2,1)} %constant.6.clone.table_ref, f32[2,128,32]{2,1,0:T(8,128)} %get-tuple-element.10.margin_ref, ...), custom_call_target="tpu_custom_call" | custom-call | tf_op jit(solution)/shard_map/last_part/pallas_call | solution.py:636
  82.0 1.3 %copy.13 = f32[128,8]{0,1:T(8,128)} copy(f32[128,8]{0,1:T(8,128)} %bitcast.15) | data formatting | bytes 8192

commit v4 on v3

--- a/solution.py
+++ b/solution.py
@@ -225,7 +225,9 @@
             if half == 0:
                 slot = slot_ref[:, pl.ds(start, BLOCK)]
                 third = lax.rem(lax.rem(slot, length) + width // 2, length)
-                pick_col = one_hot(cols, slot // length)
+                down = jnp.broadcast_to(slot // length, (8, BLOCK)).T[:, 0:1]
+                across = lax.broadcasted_iota(jnp.int32, (BLOCK, cols), 1)
+                pick_col = (across == down).astype(F32).astype(BF16)
                 pick_third = one_hot(width, third)
                 picks[step] = pick_col
                 thirds[step] = pick_third
@@ -236,7 +238,7 @@
             spread = jnp.concatenate(
                 [pick_third * values[q : q + 1] for q in range(values.shape[0])], axis=0
             )
-            acc[...] += lax.dot_general(spread, pick_col, NT, preferred_element_type=F32)
+            acc[...] += jnp.dot(spread, pick_col, preferred_element_type=F32)
             return carry
 
         lax.fori_loop(0, steps, scatter, 0)
@@ -309,7 +311,7 @@
         ],
         scratch_shapes=[
             pltpu.VMEM((count * width, cols), F32),
-            pltpu.VMEM((steps, cols, BLOCK), BF16),
+            pltpu.VMEM((steps, BLOCK, cols), BF16),
             pltpu.VMEM((steps, width, BLOCK), BF16),
             pltpu.VMEM((2, devices, cols // 2, lanes), BF16),
             pltpu.VMEM(wave_shape, BF16),
@@ -394,11 +396,18 @@
         starts = [pl.multiple_of((2 * step + u) * wide, 8) for u in range(2)]
         tiles = [mid[pl.ds(start, wide), :] for start in starts]
         got = jnp.dot(ty_ref[...], stacked(tiles), preferred_element_type=F32)
-        tiles = []
-        for u, tile in enumerate(split(got)):
-            local = v_ref[pl.ds(2 * step + u, planes, stride=n_one), :]
-            tiles.append(tile * jnp.concatenate([local] * (lanes // planes), axis=0).T)
-        back = jnp.dot(tyb_ref[...], stacked(tiles), preferred_element_type=F32)
+        local = jnp.concatenate(
+            [
+                jnp.concatenate(
+                    [v_ref[pl.ds(2 * step + u, planes, stride=n_one), :]] * (lanes // planes),
+                    axis=0,
+                ).T
+                for u in range(2)
+            ],
+            axis=1,
+        )
+        both = (got * jnp.concatenate([local, local], axis=0)).astype(BF16)
+        back = jnp.dot(tyb_ref[...], both, preferred_element_type=F32)
         for u, tile in enumerate(split(back)):
             mid_back[pl.ds(starts[u], wide), :] = tile
         return carry
@@ -560,39 +569,43 @@
                     )
                 )
 
-    def hamiltonian(step, carry):
-        add_products(
-            acc_h,
-            slab_in,
-            step,
-            lambda block: [
-                unpacked(app[b, half, block], count) for b in range(bands) for half in range(2)
-            ],
-        )
-        return carry
-
-    for g in range(groups):
-        span = pl.ds(g * each, each)
-        for mate in mates:
-            for half in range(2):
+    for half in range(2):
+
+        def hamiltonian(step, carry):
+            add_products(
+                acc_h.at[half],
+                slab_in,
+                step,
+                lambda block: [unpacked(app[b, half, block], count) for b in range(bands)],
+            )
+            return carry
+
+        for g in range(groups):
+            span = pl.ds(g * each, each)
+            for mate in mates:
                 arrived(
                     "band", mate, app.at[mate, half, span], send_b.at[mate, half, g],
                     recv_b.at[mate, half, g],
                 )
-        lax.fori_loop(g * each // 2, (g + 1) * each // 2, hamiltonian, 0)
-
-    width_h = margin_ref.shape[2]
+            lax.fori_loop(g * each // 2, (g + 1) * each // 2, hamiltonian, 0)
+
     real_rows, imag_rows = [
-        jnp.concatenate([collapse(acc_h, which, width_h), margin_ref[which]], axis=1).T
+        jnp.concatenate(
+            [collapse(acc_h.at[half], which, bands * count) for half in range(2)]
+            + [margin_ref[which]],
+            axis=1,
+        ).T
         for which in range(2)
     ]
 
     def pick(value, kind, which):
-        first = kind * bands * size + which * (count // 2)
-        return jnp.concatenate(
-            [value[first + b * count : first + b * count + count // 2] for b in range(2 * bands)],
-            axis=0,
-        )
+        firsts = [
+            (half * bands + b if kind == 0 else (bands + b) * 2 + half) * count
+            + which * (count // 2)
+            for b in range(bands)
+            for half in range(2)
+        ]
+        return jnp.concatenate([value[first : first + count // 2] for first in firsts], axis=0)
 
     pieces = []
     for kind in range(2):
@@ -645,7 +658,7 @@
             pltpu.VMEM((1, n), F32),
             pltpu.VMEM((mates, 2, steps, 16, BLOCK * count // 16), BF16),
             pltpu.VMEM(slab.shape, BF16),
-            pltpu.VMEM((mates * size * BLOCK // 128 // 128, rows * BLOCK // 64, 128), F32),
+            pltpu.VMEM((2, mates * count * BLOCK // 128 // 128, rows * BLOCK // 64, 128), F32),
             pltpu.VMEM((2 * mates * size, rows), F32),
             pltpu.VMEM((devices, share, rows), F32),
             dma,
@@ -682,7 +695,7 @@
     cx, sx = cos_sin(np.arange(n_one), signed_of(wide), n_one)
     tables = [
         np.concatenate([cx, sx], axis=1),
-        np.concatenate([cy, sy], axis=1),
+        np.block([[cy, sy], [-sy, cy]]),
         np.concatenate([cy.T, -sy.T], axis=1),
         np.concatenate([cx.T, -sx.T], axis=1),
     ]

time: 83.5 us -> 94.1 us (1.13)
  Pallas kernels: 82 us -> 92.5 us
    pallas_call x1, Pallas kernels: 22.5 us -> 29.4 us  [plane_part(): pl.pallas_call(functools.partial(plane_kernel, wide, n_one, n_two), in_sp...]
    pallas_call x1, Pallas kernels: 25.6 us -> 28.9 us  [first_part(): pl.pallas_call(functools.partial(first_kernel, sizes, wide, width), in_sp...]
where the time goes in v4:
time: 94.1 us; the launch traced here: 93.8 us
  Pallas kernels  92.5 us (98%)
  local copies, waits for them, and re-layouts  1.27 us (1%)
    pallas_call x1, Pallas kernels, last_part(): pl.pallas_call(functools.partial(last_kernel, sizes, width, groups), in_s...  34.2 us
    pallas_call x1, Pallas kernels, plane_part(): pl.pallas_call(functools.partial(plane_kernel, wide, n_one, n_two), in_sp...  29.4 us
    pallas_call x1, Pallas kernels, first_part(): pl.pallas_call(functools.partial(first_kernel, sizes, wide, width), in_sp...  28.9 us

profile of v4, /device:TPU:0, one launch (start us, length us, event | category | flops | bytes accessed | tf_op | source)
XLA Modules:
  0.0 93.8 jit_solution(9153631291721522053)
XLA Ops:
  0.0 28.9 %first_part.1 = (bf16[8,2,128,128]{3,2,1,0:T(8,128)(2,1)}, s32[8,1,256]{2,1,0:T(1,128)}, f32[2,128,32]{2,1,0:T(8,128)}) custom-call(s32[1,12288]{1,0:T(1,128)} %bitcast.13, f32[4,2,12288]{2,1,0:T(2,128)} %panel_ref.3, s32[1,256]{1,0:T(1,128)} %bitcast.17, bf16[320,512]{1,0:T(8,128)(2,1)} %constant.8.clone.table_ref, bf16[128,192,128]{2,1,0:T(8,128)(2,1)} %bitcast.10), custom_call_target="tpu_custom_call" | custom-call | tf_op jit(solution)/shard_map/first_part/pallas_call | solution.py:303
  28.9 29.4 %plane_part.1.x_ref = bf16[8,2,128,128]{3,2,1,0:T(8,128)(2,1)} custom-call(s32[2048]{0:T(1024)} %bitcast.16, bf16[8,2,128,128]{3,2,1,0:T(8,128)(2,1)} %get-tuple-element.9.x_ref, bf16[128,112]{1,0:T(8,128)(2,1)} %constant.9.clone.tx_ref, bf16[256,112]{1,0:T(8,128)(2,1)} %constant.10.clone.ty_ref, bf16[56,256]{1,0:T(8,128)(2,1)} %constant.11.clone.tyb_ref.txb_ref, ...), custom_call_target="tpu_custom_call" | custom-call | tf_op jit(solution)/shard_map/plane_part/pallas_call | solution.py:454
  58.3 34.2 %last_part.1 = f32[8,128]{1,0:T(8,128)} custom-call(s32[1,12288]{1,0:T(1,128)} %bitcast.14, f32[4,2,12288]{2,1,0:T(2,128)} %panel_ref.3, s32[1,256]{1,0:T(1,128)} %bitcast.18, bf16[8,2,128,128]{3,2,1,0:T(8,128)(2,1)} %plane_part.1.x_ref, bf16[320,512]{1,0:T(8,128)(2,1)} %constant.8.clone.table_ref, f32[2,128,32]{2,1,0:T(8,128)} %get-tuple-element.10.margin_ref, ...), custom_call_target="tpu_custom_call" | custom-call | tf_op jit(solution)/shard_map/last_part/pallas_call | solution.py:649
  92.6 1.3 %copy.13 = f32[128,8]{0,1:T(8,128)} copy(f32[128,8]{0,1:T(8,128)} %bitcast.15) | data formatting | bytes 8192
